TPU v7x, 128 devices: a whole 4x4x4 slice. The times are simulated.
128 devices in a mesh: fsdp: 4 (over z), seq: 8 (over x, core), tensor: 4 (over y).
Axes of the slice: x: 4, y: 4, z: 4, core: 2. Of those that a mesh axis runs over, the one named last changes fastest.
Arguments:
- block_input: bfloat16 [16384, 512], P(('fsdp', 'seq', 'tensor')), may hold values from -6 to 6
- cotangent: bfloat16 [16384, 512], P(('fsdp', 'seq', 'tensor')), may hold values from -6 to 6
- doc_lengths: int32 [4, 4], P('fsdp'), may hold values from 1 to 3840, as said below
- joint_weight: float32 [512, 1536], P(('fsdp', 'seq', 'tensor')), may hold values from -0.375 to 0.375
- output_weight: float32 [512, 512], P(('fsdp', 'seq', 'tensor')), may hold values from -1.5 to 1.5
- expand_weight: float32 [512, 2048], P(('fsdp', 'seq', 'tensor')), may hold values from -0.25 to 0.25
- reduce_weight: float32 [512, 2048], P(('fsdp', 'seq', 'tensor')), may hold values from -0.125 to 0.125
- joint_moment: float32 [512, 1536], P(('fsdp', 'seq', 'tensor')), may hold values from -4096 to 4096
- output_moment: float32 [512, 512], P(('fsdp', 'seq', 'tensor')), may hold values from -224 to 224
- expand_moment: float32 [512, 2048], P(('fsdp', 'seq', 'tensor')), may hold values from -224 to 224
- reduce_moment: float32 [512, 2048], P(('fsdp', 'seq', 'tensor')), may hold values from -448 to 448
- vectors: float32 [11, 512], P(None, ('fsdp', 'seq', 'tensor'))
- first_moment: float32 [11, 512], P(None, ('fsdp', 'seq', 'tensor'))
- second_moment: float32 [11, 512], P(None, ('fsdp', 'seq', 'tensor'))
Outputs:
- block_output: bfloat16 [16384, 512], P(('fsdp', 'seq', 'tensor'))
- input_grad: float32 [16384, 512], P(('fsdp', 'seq', 'tensor'))
- gradient_joint: float32 [512, 1536], P(('fsdp', 'seq', 'tensor'))
- gradient_output: float32 [512, 512], P(('fsdp', 'seq', 'tensor'))
- gradient_expand: float32 [512, 2048], P(('fsdp', 'seq', 'tensor'))
- gradient_reduce: float32 [512, 2048], P(('fsdp', 'seq', 'tensor'))
- momentum_joint: float32 [512, 1536], P(('fsdp', 'seq', 'tensor'))
- momentum_output: float32 [512, 512], P(('fsdp', 'seq', 'tensor'))
- momentum_expand: float32 [512, 2048], P(('fsdp', 'seq', 'tensor'))
- momentum_reduce: float32 [512, 2048], P(('fsdp', 'seq', 'tensor'))
- updated_joint: float32 [512, 1536], P(('fsdp', 'seq', 'tensor'))
- updated_output: float32 [512, 512], P(('fsdp', 'seq', 'tensor'))
- updated_expand: float32 [512, 2048], P(('fsdp', 'seq', 'tensor'))
- updated_reduce: float32 [512, 2048], P(('fsdp', 'seq', 'tensor'))
- vector_grad: float32 [11, 512], P(None, ('fsdp', 'seq', 'tensor'))
- second_next: float32 [11, 512], P(None, ('fsdp', 'seq', 'tensor'))
- vector_next: float32 [11, 512], P(None, ('fsdp', 'seq', 'tensor'))
Inputs may be any that keep to these rules, and one draw needn't show every extreme that they name: `doc_lengths`: each row gives the lengths of the 4 documents of one pack in order; they sum to 4096, and exactly one of them, at a place drawn from the seed, is 3840 tokens long.
All inputs are finite; a program needn't handle non-finite values.
Results may differ from a plain program's by a relative error of at most 0.014.
The roundings to bfloat16 on the way count: a program that leaves them out, or rounds other values in their place, can miss the bound.
Values may be sent and summed in bfloat16 or wider, within the bound.
A program may use at most 128 MiB of HBM per device.

v0:
```python
import math

import jax
import jax.numpy as jnp
from jax import lax
from jax.sharding import PartitionSpec as P

D = 512
HEADS = 8
FF = 2048
ROT = 16
HD = 64
SWEEPS = 5
STEP = 10
PADW = 2048


norm_epsilon = 1e-05
masked_score = -1e30
newton_first = 3.4445
newton_second = -4.775
newton_third = 2.0315
beta_first = 0.9
beta_second = 0.95
adam_epsilon = 1e-08
vector_rate = 0.2
muon_rate = 0.25
muon_beta = 0.95
muon_decay = 0.01


def for_sending(shard):

    def short(part):
        return part.astype(jnp.bfloat16) if part.dtype == jnp.float32 else part

    return jax.tree.map(short, shard)


def doc_positions(row_index, lengths):
    finish = jnp.cumsum(lengths, dtype=jnp.int32)
    passed = row_index[:, None] >= finish[None, :]
    documents = jnp.sum(passed.astype(jnp.int32), axis=1, dtype=jnp.int32)
    starts = jnp.sum(jnp.where(passed, lengths[None, :], 0), axis=1, dtype=jnp.int32)
    return (documents, row_index - starts)


def rotate(tensor, position, rot_dims, direction):
    half_dims = rot_dims // 2
    frequency = 10000.0 ** (-(jnp.arange(half_dims, dtype=jnp.float32) * 2.0) / rot_dims)
    angles = position.astype(jnp.float32)[:, None] * frequency[None, :]
    cosine = jnp.cos(angles)[:, None, :]
    sine = direction * jnp.sin(angles)[:, None, :]
    first = tensor[..., :half_dims]
    second = tensor[..., half_dims:rot_dims]
    return jnp.concatenate(
        [first * cosine - second * sine, second * cosine + first * sine, tensor[..., rot_dims:]],
        axis=-1,
    )


def layer_norm(values, norm_gain, norm_shift):
    mean_value = jnp.mean(values, axis=-1, keepdims=True)
    centred = values - mean_value
    variance = jnp.mean(centred * centred, axis=-1, keepdims=True)
    return centred * lax.rsqrt(variance + norm_epsilon) * norm_gain + norm_shift


def orthogonalize(matrix):
    highest = lax.Precision.HIGHEST
    current = matrix / (jnp.sqrt(jnp.sum(matrix * matrix)) + 1e-07)
    for iteration in range(SWEEPS):
        gram_matrix = jnp.dot(current, current.T, precision=highest)
        mixture = newton_second * gram_matrix + newton_third * jnp.dot(
            gram_matrix, gram_matrix, precision=highest
        )
        current = newton_first * current + jnp.dot(mixture, current, precision=highest)
    return current


def contract_rows(left, right):
    return lax.dot_general(
        left, right, (((0,), (0,)), ((), ())), preferred_element_type=jnp.float32
    )


def contract_cols(left, right):
    return lax.dot_general(
        left, right, (((1,), (1,)), ((), ())), preferred_element_type=jnp.float32
    )


def shards(
    block_input,
    cotangent,
    doc_lengths,
    joint_weight,
    output_weight,
    expand_weight,
    reduce_weight,
    joint_moment,
    output_moment,
    expand_moment,
    reduce_moment,
    vectors,
    first_moment,
    second_moment,
):
    seq_count = lax.axis_size("seq")
    tensor_count = lax.axis_size("tensor")
    group_count = lax.axis_size("fsdp")
    seq_index = lax.axis_index("seq")
    tensor_index = lax.axis_index("tensor")
    local_rows = block_input.shape[0]
    heads_here = HEADS // seq_count
    hidden_local = FF // tensor_count
    scaling = HD ** (-0.5)
    gathered = (
        lax.all_gather(
            joint_weight.astype(jnp.bfloat16), ("fsdp", "seq", "tensor"), axis=0, tiled=True
        ),
        lax.all_gather(
            output_weight.astype(jnp.bfloat16), ("fsdp", "seq", "tensor"), axis=0, tiled=True
        ),
        lax.all_gather(
            expand_weight.astype(jnp.bfloat16), ("fsdp", "seq", "tensor"), axis=0, tiled=True
        ),
        lax.all_gather(
            reduce_weight.astype(jnp.bfloat16), ("fsdp", "seq", "tensor"), axis=0, tiled=True
        ),
        lax.all_gather(vectors.astype(jnp.bfloat16), ("fsdp", "seq", "tensor"), axis=1, tiled=True),
    )
    joint_full, output_full, expand_full, reduce_full, vector_full = gathered
    vector_values = vector_full.astype(jnp.float32)
    norm_gain = vector_values[0]
    norm_shift = vector_values[1]
    query_bias = vector_values[2]
    key_bias = vector_values[3]
    value_bias = vector_values[4]
    output_bias = vector_values[5]
    reduce_bias = vector_values[6]
    expand_bias = vector_values[7:].reshape(FF)
    expand_local = lax.dynamic_slice_in_dim(
        expand_full, tensor_index * hidden_local, hidden_local, 1
    )
    reduce_local = lax.dynamic_slice_in_dim(
        reduce_full, tensor_index * hidden_local, hidden_local, 1
    )
    bias_local = lax.dynamic_slice_in_dim(expand_bias, tensor_index * hidden_local, hidden_local, 0)
    inputs = block_input.astype(jnp.float32)
    normed = layer_norm(inputs, norm_gain, norm_shift)
    normed_low = normed.astype(jnp.bfloat16)
    rows_all, cot_rows = (
        lax.all_gather(normed_low, "tensor", axis=0, tiled=True),
        lax.all_gather(cotangent, "tensor", axis=0, tiled=True),
    )
    lengths = doc_lengths[0]
    own_index = (seq_index * tensor_count + tensor_index) * local_rows + jnp.arange(
        local_rows, dtype=jnp.int32
    )
    own_pos = doc_positions(own_index, lengths)[1]
    query_raw = (
        jnp.dot(normed_low, joint_full[:, :D], preferred_element_type=jnp.float32) + query_bias
    )
    query_low = rotate(query_raw.reshape(local_rows, HEADS, HD), own_pos, ROT, 1.0).astype(
        jnp.bfloat16
    )
    key_source_pos = doc_positions(own_index, lengths)[1]
    pair_raw = jnp.dot(normed_low, joint_full[:, D:], preferred_element_type=jnp.float32)
    key_raw = pair_raw[:, :D] + key_bias
    key_low = rotate(key_raw.reshape(-1, HEADS, HD), key_source_pos, ROT, 1.0).astype(jnp.bfloat16)
    value_low = (pair_raw[:, D:] + value_bias).reshape(-1, HEADS, HD).astype(jnp.bfloat16)
    query_heads, key_heads, value_heads = (
        lax.all_to_all(query_low, "seq", split_axis=1, concat_axis=0, tiled=True),
        lax.all_to_all(key_low, "seq", split_axis=1, concat_axis=0, tiled=True),
        lax.all_to_all(value_low, "seq", split_axis=1, concat_axis=0, tiled=True),
    )
    key_heads, value_heads = (
        lax.all_gather(key_heads, "tensor", axis=0, tiled=True),
        lax.all_gather(value_heads, "tensor", axis=0, tiled=True),
    )
    tensor_ids = jnp.arange(tensor_count, dtype=jnp.int32)[:, None, None]
    seq_ids = jnp.arange(seq_count, dtype=jnp.int32)[None, :, None]
    row_ids = jnp.arange(local_rows, dtype=jnp.int32)[None, None, :]
    key_index = ((seq_ids * tensor_count + tensor_ids) * local_rows + row_ids).reshape(-1)
    key_doc = doc_positions(key_index, lengths)[0]
    query_index = (
        (jnp.arange(seq_count, dtype=jnp.int32)[:, None] * tensor_count + tensor_index) * local_rows
        + jnp.arange(local_rows, dtype=jnp.int32)[None, :]
    ).reshape(-1)
    query_doc = doc_positions(query_index, lengths)[0]
    query_count = query_heads.shape[0]
    block_rows = math.gcd(query_count, 512)
    block_count = query_count // block_rows
    query_blocks = query_heads.reshape(block_count, block_rows, heads_here, HD)
    qdoc_blocks = query_doc.reshape(block_count, block_rows)
    qindex_blocks = query_index.reshape(block_count, block_rows)

    def block_scores(query_block, doc_block, index_block):
        scores = (
            jnp.einsum("qhd,khd->hqk", query_block, key_heads, preferred_element_type=jnp.float32)
            * scaling
        )
        allowed = (doc_block[:, None] == key_doc[None, :]) & (
            key_index[None, :] <= index_block[:, None]
        )
        return jnp.where(allowed[None], scores, masked_score)

    def forward_block(packed):
        query_block, doc_block, index_block = packed
        scores = block_scores(query_block, doc_block, index_block)
        row_max = jnp.max(scores, axis=-1, keepdims=True)
        exponent = jnp.exp(scores - row_max)
        row_sum = jnp.sum(exponent, axis=-1, keepdims=True)
        probability = (exponent / row_sum).astype(jnp.bfloat16)
        attended = jnp.einsum(
            "hqk,khd->qhd", probability, value_heads, preferred_element_type=jnp.float32
        )
        return (attended.astype(jnp.bfloat16), (row_max + jnp.log(row_sum))[..., 0])

    attended_blocks, log_totals = lax.map(forward_block, (query_blocks, qdoc_blocks, qindex_blocks))
    token_out = lax.all_to_all(
        attended_blocks.reshape(query_count, heads_here, HD),
        "seq",
        split_axis=0,
        concat_axis=1,
        tiled=True,
    )
    token_out = token_out.reshape(local_rows, D)
    attention_term = jnp.dot(token_out, output_full, preferred_element_type=jnp.float32)
    hidden_pre = jnp.dot(rows_all, expand_local, preferred_element_type=jnp.float32) + bias_local

    def activation(pre_values):
        return jax.nn.gelu(pre_values, approximate=True)

    hidden_act, gelu_back = jax.vjp(activation, hidden_pre)
    hidden_low = hidden_act.astype(jnp.bfloat16)
    feed_term = contract_cols(hidden_low, reduce_local)
    own_slice = (
        lax.dynamic_slice_in_dim(feed_term, tensor_index * local_rows, local_rows, 0)
        + attention_term
    )
    combined = lax.dynamic_update_slice_in_dim(feed_term, own_slice, tensor_index * local_rows, 0)
    summed = lax.psum_scatter(
        combined.astype(jnp.bfloat16), "tensor", scatter_dimension=0, tiled=True
    ).astype(jnp.float32)
    block_output = (inputs + summed + output_bias + reduce_bias).astype(jnp.bfloat16)
    upstream = cotangent.astype(jnp.float32)
    output_grad_full = contract_rows(token_out, cotangent)
    token_grad = (
        contract_cols(cotangent, output_full).astype(jnp.bfloat16).reshape(local_rows, HEADS, HD)
    )
    grad_heads = lax.all_to_all(token_grad, "seq", split_axis=1, concat_axis=0, tiled=True)
    hidden_grad = jnp.dot(cot_rows, reduce_local, preferred_element_type=jnp.float32)
    pre_grad_low = gelu_back(hidden_grad)[0].astype(jnp.bfloat16)
    reduce_grad_local = contract_rows(cot_rows, hidden_low)
    expand_grad_local = contract_rows(rows_all, pre_grad_low)
    expand_bias_local = jnp.sum(pre_grad_low.astype(jnp.float32), axis=0)
    row_grad = contract_cols(pre_grad_low, expand_local)
    normed_grad_feed = lax.psum_scatter(
        row_grad.astype(jnp.bfloat16), "tensor", scatter_dimension=0, tiled=True
    ).astype(jnp.float32)
    grad_blocks = grad_heads.reshape(block_count, block_rows, heads_here, HD)

    def backward_block(carried, packed):
        key_total, value_total = carried
        query_block, doc_block, index_block, grad_block, lse_block = packed
        scores = block_scores(query_block, doc_block, index_block)
        probability = jnp.exp(scores - lse_block[..., None])
        prob_grad = jnp.einsum(
            "qhd,khd->hqk", grad_block, value_heads, preferred_element_type=jnp.float32
        )
        centre = jnp.sum(probability * prob_grad, axis=-1, keepdims=True)
        score_grad = (probability * (prob_grad - centre)).astype(jnp.bfloat16)
        query_grad = (
            jnp.einsum("hqk,khd->qhd", score_grad, key_heads, preferred_element_type=jnp.float32)
            * scaling
        )
        key_total = (
            key_total
            + jnp.einsum(
                "hqk,qhd->khd", score_grad, query_block, preferred_element_type=jnp.float32
            )
            * scaling
        )
        value_total = value_total + jnp.einsum(
            "hqk,qhd->khd",
            probability.astype(jnp.bfloat16),
            grad_block,
            preferred_element_type=jnp.float32,
        )
        return ((key_total, value_total), query_grad)

    empty_keys = jnp.zeros(key_heads.shape, jnp.float32)
    key_value_totals, query_grads = lax.scan(
        backward_block,
        (empty_keys, empty_keys),
        (query_blocks, qdoc_blocks, qindex_blocks, grad_blocks, log_totals),
    )
    key_sum, value_sum = (
        lax.psum_scatter(
            key_value_totals[0].astype(jnp.bfloat16), "tensor", scatter_dimension=0, tiled=True
        ).astype(jnp.float32),
        lax.psum_scatter(
            key_value_totals[1].astype(jnp.bfloat16), "tensor", scatter_dimension=0, tiled=True
        ).astype(jnp.float32),
    )
    query_back, key_back, value_back = (
        lax.all_to_all(
            query_grads.reshape(query_count, heads_here, HD).astype(jnp.bfloat16),
            "seq",
            split_axis=0,
            concat_axis=1,
            tiled=True,
        ),
        lax.all_to_all(
            key_sum.astype(jnp.bfloat16), "seq", split_axis=0, concat_axis=1, tiled=True
        ),
        lax.all_to_all(
            value_sum.astype(jnp.bfloat16), "seq", split_axis=0, concat_axis=1, tiled=True
        ),
    )
    query_raw_grad = (
        rotate(query_back.astype(jnp.float32), own_pos, ROT, -1.0)
        .astype(jnp.bfloat16)
        .reshape(local_rows, D)
    )
    key_raw_grad = (
        rotate(key_back.astype(jnp.float32), own_pos, ROT, -1.0)
        .astype(jnp.bfloat16)
        .reshape(local_rows, D)
    )
    value_raw_grad = value_back.reshape(local_rows, D)
    joint_out_grad = jnp.concatenate([query_raw_grad, key_raw_grad, value_raw_grad], axis=1)
    joint_grad_full = contract_rows(normed_low, joint_out_grad)
    normed_grad = contract_cols(joint_out_grad, joint_full) + normed_grad_feed
    norm_pair = jax.vjp(layer_norm, inputs, norm_gain, norm_shift)
    input_part, gain_grad, shift_grad = norm_pair[1](normed_grad)
    input_grad = upstream + input_part
    upstream_sum = jnp.sum(upstream, axis=0)
    expand_bias_full = lax.dynamic_update_slice_in_dim(
        jnp.zeros((FF,), jnp.float32), expand_bias_local, tensor_index * hidden_local, 0
    )
    vector_rows = jnp.concatenate(
        [
            jnp.stack(
                [
                    gain_grad,
                    shift_grad,
                    jnp.sum(query_raw_grad.astype(jnp.float32), axis=0),
                    jnp.sum(key_raw_grad.astype(jnp.float32), axis=0),
                    jnp.sum(value_raw_grad.astype(jnp.float32), axis=0),
                    upstream_sum,
                    upstream_sum,
                ]
            ),
            expand_bias_full.reshape(FF // D, D),
        ],
        axis=0,
    )
    expand_grad_full = lax.dynamic_update_slice_in_dim(
        jnp.zeros((D, FF), jnp.float32), expand_grad_local, tensor_index * hidden_local, 1
    )
    reduce_grad_full = lax.dynamic_update_slice_in_dim(
        jnp.zeros((D, FF), jnp.float32), reduce_grad_local, tensor_index * hidden_local, 1
    )
    joint_grad, output_grad, expand_grad, reduce_grad, vector_grad = (
        lax.psum_scatter(
            joint_grad_full, ("fsdp", "seq", "tensor"), scatter_dimension=0, tiled=True
        ),
        lax.psum_scatter(
            output_grad_full, ("fsdp", "seq", "tensor"), scatter_dimension=0, tiled=True
        ),
        lax.psum_scatter(
            expand_grad_full, ("fsdp", "seq", "tensor"), scatter_dimension=0, tiled=True
        ),
        lax.psum_scatter(
            reduce_grad_full, ("fsdp", "seq", "tensor"), scatter_dimension=0, tiled=True
        ),
        lax.psum_scatter(vector_rows, ("fsdp", "seq", "tensor"), scatter_dimension=1, tiled=True),
    )
    masters = (joint_weight, output_weight, expand_weight, reduce_weight)
    moments = (joint_moment, output_moment, expand_moment, reduce_moment)
    gradients = (joint_grad, output_grad, expand_grad, reduce_grad)
    momenta = [muon_beta * moments[member] + gradients[member] for member in range(4)]

    def widen_matrix(matrix):
        return jnp.pad(matrix, ((0, 0), (0, PADW - matrix.shape[1])))

    stacked = jnp.stack([widen_matrix(matrix) for matrix in momenta])
    received = lax.all_to_all(
        stacked.astype(jnp.bfloat16), "fsdp", split_axis=0, concat_axis=0, tiled=True
    ).astype(stacked.dtype)
    every_row = lax.all_gather(
        received[None].astype(jnp.bfloat16), ("seq", "tensor"), axis=0, tiled=True
    ).astype(jnp.float32)
    whole_matrix = every_row.transpose(1, 0, 2, 3).reshape(-1, PADW)
    orthogonal = orthogonalize(whole_matrix)
    piece_rows = stacked.shape[1]
    all_pieces = orthogonal.reshape(group_count, seq_count * tensor_count, piece_rows, PADW)
    own_pieces = lax.dynamic_index_in_dim(
        all_pieces, seq_index * tensor_count + tensor_index, 1, keepdims=False
    )
    returned = lax.all_to_all(
        for_sending(own_pieces), "fsdp", split_axis=0, concat_axis=0, tiled=True
    ).astype(own_pieces.dtype)
    widths = (3 * D, D, FF, FF)
    updated = []
    for member in range(4):
        column_width = widths[member]
        factor = muon_rate * 0.2 * math.sqrt(max(D, column_width))
        updated.append(
            masters[member] * (1.0 - muon_rate * muon_decay)
            - factor * returned[member][:, :column_width]
        )
    first_next = beta_first * first_moment + (1.0 - beta_first) * vector_grad
    second_next = beta_second * second_moment + (1.0 - beta_second) * vector_grad * vector_grad
    first_hat = first_next / (1.0 - beta_first**STEP)
    second_hat = second_next / (1.0 - beta_second**STEP)
    vector_next = vectors - vector_rate * first_hat / (jnp.sqrt(second_hat) + adam_epsilon)
    return (
        block_output,
        input_grad,
        joint_grad,
        output_grad,
        expand_grad,
        reduce_grad,
        momenta[0],
        momenta[1],
        momenta[2],
        momenta[3],
        updated[0],
        updated[1],
        updated[2],
        updated[3],
        vector_grad,
        second_next,
        vector_next,
    )


def solution(mesh):
    return jax.shard_map(
        shards,
        mesh=mesh,
        in_specs=(
            P(("fsdp", "seq", "tensor"), None),
            P(("fsdp", "seq", "tensor"), None),
            P("fsdp", None),
            P(("fsdp", "seq", "tensor"), None),
            P(("fsdp", "seq", "tensor"), None),
            P(("fsdp", "seq", "tensor"), None),
            P(("fsdp", "seq", "tensor"), None),
            P(("fsdp", "seq", "tensor"), None),
            P(("fsdp", "seq", "tensor"), None),
            P(("fsdp", "seq", "tensor"), None),
            P(("fsdp", "seq", "tensor"), None),
            P(None, ("fsdp", "seq", "tensor")),
            P(None, ("fsdp", "seq", "tensor")),
            P(None, ("fsdp", "seq", "tensor")),
        ),
        out_specs=(
            P(("fsdp", "seq", "tensor"), None),
            P(("fsdp", "seq", "tensor"), None),
            P(("fsdp", "seq", "tensor"), None),
            P(("fsdp", "seq", "tensor"), None),
            P(("fsdp", "seq", "tensor"), None),
            P(("fsdp", "seq", "tensor"), None),
            P(("fsdp", "seq", "tensor"), None),
            P(("fsdp", "seq", "tensor"), None),
            P(("fsdp", "seq", "tensor"), None),
            P(("fsdp", "seq", "tensor"), None),
            P(("fsdp", "seq", "tensor"), None),
            P(("fsdp", "seq", "tensor"), None),
            P(("fsdp", "seq", "tensor"), None),
            P(("fsdp", "seq", "tensor"), None),
            P(None, ("fsdp", "seq", "tensor")),
            P(None, ("fsdp", "seq", "tensor")),
            P(None, ("fsdp", "seq", "tensor")),
        ),
        check_vma=False,
    )
```

profile of v0, /device:TPU:1, one launch (start us, length us, event | category | flops | bytes accessed | tf_op | source)
XLA Modules:
  0.0 830.2 jit_solution(1889625574245252339)
XLA Ops:
  10.8 55.2 %all-gather.5 = bf16[128,4,512]{2,1,0:T(4,128)(2,1)S(1)} all-gather(bf16[1,4,512]{2,1,0:T(4,128)(2,1)S(1)} %convert_bitcast_fusion.7), channel_id=1, replica_groups=mesh['fsdp'=4,'seq'=8,'tensor'=4] {'fsdp','seq','tensor'}, dimensions={0}, use_global_device_ids=true | all-gather | bytes 528384 | tf_op jit(solution)/shard_map/all_gather | solution.py:122
  75.6 49.0 %all-gather.1 = bf16[128,4,11]{2,1,0:T(4,128)(2,1)S(1)} all-gather(bf16[1,4,11]{2,1,0:T(4,128)(2,1)S(1)} %convert_bitcast_fusion.8), channel_id=1, replica_groups=mesh['fsdp'=4,'seq'=8,'tensor'=4] {'fsdp','seq','tensor'}, dimensions={0}, use_global_device_ids=true | all-gather | bytes 11352 | tf_op jit(solution)/shard_map/all_gather | solution.py:131
  130.5 12.3 %all_gather.31 = bf16[512,512]{1,0:T(8,128)(2,1)} all-gather(bf16[128,512]{1,0:T(8,128)(2,1)S(1)} %fusion.65), channel_id=1, replica_groups=mesh['fsdp'=4,'seq'=8,'tensor'=4] {'tensor'}, dimensions={0}, use_global_device_ids=true | all-gather | bytes 655360 | tf_op jit(solution)/shard_map/all_gather | solution.py:154
  178.8 10.9 %all_gather.35 = bf16[4096,1,64]{0,2,1:T(8,128)(2,1)S(1)} all-gather(bf16[1024,1,64]{0,2,1:T(8,128)(2,1)S(1)} %copy_bitcast_fusion.4), channel_id=1, replica_groups=mesh['fsdp'=4,'seq'=8,'tensor'=4] {'tensor'}, dimensions={0}, use_global_device_ids=true | all-gather | bytes 655360 | tf_op jit(solution)/shard_map/all_gather | solution.py:179
  189.8 9.9 %all_gather.36 = bf16[4096,1,64]{0,2,1:T(8,128)(2,1)S(1)} all-gather(bf16[1024,1,64]{0,2,1:T(8,128)(2,1)S(1)} %copy_bitcast_fusion.3), channel_id=1, replica_groups=mesh['fsdp'=4,'seq'=8,'tensor'=4] {'tensor'}, dimensions={0}, use_global_device_ids=true | all-gather | bytes 655360 | tf_op jit(solution)/shard_map/all_gather | solution.py:180
  199.7 14.4 %while.28 = (s32[]{:T(128)}, bf16[2,512,1,64]{1,3,2,0:T(8,128)(2,1)}, f32[2,1,512]{2,1,0:T(1,128)S(1)}, s32[2,512]{1,0:T(2,128)S(1)}, s32[4096]{0:T(1024)}, /*in...) while((s32[]{:T(128)}, ...), condition=%wide.region_9.10_spmd.clone, body=%wide.region_6.9_spmd.clone.sunk | while | flops 559975936 | bytes 26428152 | solution.py:221
  214.1 53.7 %while.29 = (s32[]{:T(128)}, f32[4096,1,64]{0,2,1:T(8,128)S(1)}, f32[4096,1,64]{0,2,1:T(8,128)S(1)}, bf16[2,512,1,64]{1,3,2,0:T(8,128)(2,1)}, bf16[2,512,1,64]{1...) while((s32[]{:T(128)}, f32[4096,1,64]{0,2,1:T(8,128)S(1)}, ...), condition=%wide.region_13.14_spmd.clone, body=%wide.region_11.13_spmd.clone.sunk | while | flops 1368690176 | bytes 120592840 | solution.py:295
  221.2 9.9 %multiply_convert_fusion.5 = bf16[512,4096]{1,0:T(8,128)(2,1)} fusion(f32[512,4096]{1,0:T(8,128)} %get-tuple-element.724, f32[512,4096]{1,0:T(8,128)} %copy-done.1, f32[512]{0:T(512)S(1)} %get-tuple-element.725), kind=kLoop, calls=%fused_computation.20.clone.1 | loop fusion | flops 6291456 | bytes 20973568 | tf_op jit(solution)/shard_map/while/body/eval_jaxpr/convert_element_type | solution.py:274
  248.1 9.9 %multiply_convert_fusion.5 = bf16[512,4096]{1,0:T(8,128)(2,1)} fusion(f32[512,4096]{1,0:T(8,128)} %get-tuple-element.724, f32[512,4096]{1,0:T(8,128)} %copy-done.1, f32[512]{0:T(512)S(1)} %get-tuple-element.725), kind=kLoop, calls=%fused_computation.20.clone.1 | loop fusion | flops 6291456 | bytes 20973568 | tf_op jit(solution)/shard_map/while/body/eval_jaxpr/convert_element_type | solution.py:274
  273.2 10.4 %all-to-all-start.5 = ((bf16[8,2,4096]{2,1,0:T(2,128)(2,1)}), bf16[8,2,4096]{2,1,0:T(2,128)(2,1)S(1)}, u32[]{:S(2)}, u32[]{:S(2)}) async-start(bf16[8,2,4096]{2,1,0:T(2,128)(2,1)} %reshape.517), calls=%async_computation.6 | async-start | bytes 262144 | tf_op jit(solution)/shard_map/all_to_all | solution.py:309
  283.7 12.1 %all_gather.38 = bf16[512,512]{1,0:T(8,128)(2,1)} all-gather(bf16[128,512]{1,0:T(8,128)(2,1)S(1)} %copy-done.13), channel_id=1, replica_groups=mesh['fsdp'=4,'seq'=8,'tensor'=4] {'tensor'}, dimensions={0}, use_global_device_ids=true | all-gather | bytes 655360 | tf_op jit(solution)/shard_map/all_gather | solution.py:155
  344.1 58.3 %all-reduce.16.cloned.1.call-done = (bf16[4096,1,64]{2,1,0:T(2,128)(2,1)}, bf16[4096,1,64]{2,1,0:T(2,128)(2,1)}) async-done(((bf16[4096,1,64]{2,1,0:T(2,128)(2,1)}, bf16[4096,1,64]{2,1,0:T(2,128)(2,1)}), (bf16[4096,1,64]{2,1,0:T(2,128)(2,1)}, bf16[4096,1,64]{2,1,0:T(2,128)(2,1)})) %all-reduce.16.cloned.1.call-update) | async-done | bytes 1048592
  436.3 162.1 %all-reduce.14.cloned.1.call-done = (f32[512,1536]{1,0:T(8,128)}, f32[512,512]{1,0:T(8,128)}, f32[512,2048]{1,0:T(8,128)}, f32[512,2048]{1,0:T(8,128)}) async-done(((f32[512,1536]{1,0:T(8,128)}, f32[512,512]{1,0:T(8,128)}, f32[512,2048]{1,0:T(8,128)}, f32[512,2048]{1,0:T(8,128)}), (f32[512,1536]{1,0:T(8,128)}, f32[512,512]{1,0:T(8,128)}, f32[512,2048]{1,0:T(8,128)}, ...) | async-done | bytes 12582928
  604.3 7.7 all_to_all.124
  620.7 21.4 %reduce-scatter.4.cloned.1.call-done = bf16[128,512]{1,0:T(8,128)(2,1)} async-done(((bf16[512,512]{1,0:T(8,128)(2,1)}), bf16[128,512]{1,0:T(8,128)(2,1)}) %reduce-scatter.4.cloned.1.call-update) | async-done | bytes 131088 | tf_op jit(solution)/shard_map/reduce_scatter | solution.py:244
  644.1 66.5 %all-reduce.8 = f32[11,512]{1,0:T(8,128)S(1)} all-reduce(f32[11,512]{1,0:T(8,128)S(1)} %concatenate.25), channel_id=11, replica_groups=mesh['fsdp'=4,'seq'=8,'tensor'=4] {'fsdp','seq','tensor'}, use_global_device_ids=true, to_apply=%region_31.32.clone | all-reduce | flops 5632 | bytes 45056
  725.6 9.9 %fusion.97 = f32[512,512]{1,0:T(8,128)S(1)} fusion(f32[512,2048]{1,0:T(8,128)} %div.70), kind=kOutput, calls=%fused_computation.224 | convolution fusion | flops 6442450944 | bytes 5242880 | tf_op jit(solution)/shard_map/dot_general | solution.py:73
  744.4 7.1 fusion.98
  753.4 6.9 multiply_add_fusion.3
  760.4 7.1 fusion.99
  769.4 7.4 multiply_add_fusion.2
  785.6 7.1 multiply_add_fusion.1
  792.7 7.1 fusion.101
  801.7 8.2 multiply_add_fusion
  (333 shorter events, 256.4 us)
Async XLA Ops:
  7.2 138.2 %all-gather.17.cloned.1.call-start = ((), (), s32[]{:S(2)}) async-start(), calls=%async_computation.17 | async-start | bytes 1585152 | tf_op jit(solution)/shard_map/all_gather | solution.py:119
  8.6 313.3 %all-gather.13.cloned.1.call-start = ((), (), s32[]{:S(2)}) async-start(), calls=%async_computation.15 | async-start | bytes 2113536 | tf_op jit(solution)/shard_map/all_gather | solution.py:125
  68.2 84.8 %all-to-all-start.4 = ((bf16[128,8,64]{0,2,1:T(8,128)(2,1)}), bf16[128,8,64]{0,2,1:T(8,128)(2,1)S(1)}, u32[]{:S(2)}, u32[]{:S(2)}) async-start(bf16[128,8,64]{0,2,1:T(8,128)(2,1)} %bitcast.32), calls=%async_computation.5 | async-start | bytes 262144 | tf_op jit(solution)/shard_map/all_to_all | solution.py:253
  73.4 257.9 %all-gather.15.cloned.1.call-start = ((), (), s32[]{:S(2)}) async-start(), calls=%async_computation.16 | async-start | bytes 2113536 | tf_op jit(solution)/shard_map/all_gather | solution.py:128
  153.0 12.2 %all-to-all-start = ((bf16[128,8,64]{0,2,1:T(8,128)(2,1)}), bf16[128,8,64]{0,2,1:T(8,128)(2,1)S(1)}, u32[]{:S(2)}, u32[]{:S(2)}) async-start(bf16[128,8,64]{0,2,1:T(8,128)(2,1)} %pad_maximum_fusion.3), calls=%async_computation | async-start | bytes 262144 | tf_op jit(solution)/shard_map/all_to_all | solution.py:174
  165.3 9.4 %all-to-all-start.1 = ((bf16[128,8,64]{0,2,1:T(8,128)(2,1)}), bf16[128,8,64]{0,2,1:T(8,128)(2,1)S(1)}, u32[]{:S(2)}, u32[]{:S(2)}) async-start(bf16[128,8,64]{0,2,1:T(8,128)(2,1)} %pad_maximum_fusion.4), calls=%async_computation.1 | async-start | bytes 262144 | tf_op jit(solution)/shard_map/all_to_all | solution.py:175
  174.7 15.1 %all-to-all-start.2 = ((bf16[128,8,64]{0,2,1:T(8,128)(2,1)}), bf16[128,8,64]{0,2,1:T(8,128)(2,1)S(1)}, u32[]{:S(2)}, u32[]{:S(2)}) async-start(bf16[128,8,64]{0,2,1:T(8,128)(2,1)} %bitcast.24), calls=%async_computation.2 | async-start | bytes 262144 | tf_op jit(solution)/shard_map/all_to_all | solution.py:176
  273.2 34.9 %all-to-all-start.5 = ((bf16[8,2,4096]{2,1,0:T(2,128)(2,1)}), bf16[8,2,4096]{2,1,0:T(2,128)(2,1)S(1)}, u32[]{:S(2)}, u32[]{:S(2)}) async-start(bf16[8,2,4096]{2,1,0:T(2,128)(2,1)} %reshape.517), calls=%async_computation.6 | async-start | bytes 262144 | tf_op jit(solution)/shard_map/all_to_all | solution.py:309
  283.6 118.7 %all-reduce.16.cloned.1.call-start = ((), (), s32[]{:S(2)}) async-start(), calls=%async_computation.19 | async-start | bytes 8388608
  308.1 11.7 %all-to-all-start.3 = ((bf16[8,2,4096]{2,1,0:T(2,128)(2,1)}), bf16[8,2,4096]{2,1,0:T(2,128)(2,1)S(1)}, u32[]{:S(2)}, u32[]{:S(2)}) async-start(bf16[8,2,4096]{2,1,0:T(2,128)(2,1)} %reshape.511), calls=%async_computation.3 | async-start | bytes 262144 | tf_op jit(solution)/shard_map/all_to_all | solution.py:222
  407.1 10.5 %all-to-all-start.6 = ((bf16[8,2,4096]{2,1,0:T(2,128)(2,1)}), bf16[8,2,4096]{2,1,0:T(2,128)(2,1)S(1)}, u32[]{:S(2)}, u32[]{:S(2)}) async-start(bf16[8,2,4096]{2,1,0:T(2,128)(2,1)} %reshape.515), calls=%async_computation.7 | async-start | bytes 262144 | tf_op jit(solution)/shard_map/all_to_all | solution.py:316
  417.6 9.6 %all-to-all-start.7 = ((bf16[8,2,4096]{2,1,0:T(2,128)(2,1)}), bf16[8,2,4096]{2,1,0:T(2,128)(2,1)S(1)}, u32[]{:S(2)}, u32[]{:S(2)}) async-start(bf16[8,2,4096]{2,1,0:T(2,128)(2,1)} %reshape.513), calls=%async_computation.8 | async-start | bytes 262144 | tf_op jit(solution)/shard_map/all_to_all | solution.py:319
  422.0 176.4 %all-reduce.14.cloned.1.call-start = ((), (), s32[]{:S(2)}) async-start(), calls=%async_computation.18 | async-start | bytes 25165824
  430.6 188.0 %reduce-scatter.6.cloned.1.call-start = ((), (), s32[]{:S(2)}) async-start(), calls=%async_computation.13 | async-start | bytes 655360 | tf_op jit(solution)/shard_map/reduce_scatter | solution.py:260
  433.0 185.6 %copy-start.4 = (bf16[512,1536]{1,0:T(8,128)(2,1)S(1)}, bf16[512,1536]{1,0:T(8,128)(2,1)}, u32[]{:S(2)}) copy-start(bf16[512,1536]{1,0:T(8,128)(2,1)} %reshape.494) | copy-start | bytes 4718596
  433.0 185.6 %copy-start.12 = (bf16[128,512]{1,0:T(8,128)(2,1)S(1)}, bf16[128,512]{1,0:T(8,128)(2,1)}, u32[]{:S(2)}) copy-start(bf16[128,512]{1,0:T(8,128)(2,1)} %param.18) | copy-start | bytes 393220
  433.0 185.6 %copy-start.29 = (f32[1,512]{1,0:T(1,128)S(1)}, f32[1,512]{1,0:T(1,128)}, u32[]{:S(2)}) copy-start(f32[1,512]{1,0:T(1,128)} %copy-done.28) | copy-start | bytes 6148
  433.0 185.6 %copy-start.34 = (f32[128]{0:T(128)S(1)}, f32[128]{0:T(128)}, u32[]{:S(2)}) copy-start(f32[128]{0:T(128)} %copy-done.33) | copy-start | bytes 1540
  433.0 209.1 %reduce-scatter.4.cloned.1.call-start = ((), (), s32[]{:S(2)}) async-start(), calls=%async_computation.12 | async-start | bytes 655360 | tf_op jit(solution)/shard_map/reduce_scatter | solution.py:244
  435.4 185.1 %copy-start.41 = (f32[128]{0:T(128)S(1)}, f32[128]{0:T(128)}, u32[]{:S(2)}) copy-start(f32[128]{0:T(128)} %copy-done.40) | copy-start | bytes 1540
  435.4 206.8 %copy-start.35 = (f32[1,512]{1,0:T(1,128)S(1)}, f32[1,512]{1,0:T(1,128)}, u32[]{:S(2)}) copy-start(f32[1,512]{1,0:T(1,128)} %get-tuple-element.551) | copy-start | bytes 6148
  435.4 206.8 %copy-start.36 = (f32[1,512]{1,0:T(1,128)S(1)}, f32[1,512]{1,0:T(1,128)}, u32[]{:S(2)}) copy-start(f32[1,512]{1,0:T(1,128)} %get-tuple-element.552) | copy-start | bytes 6148
  436.3 274.5 %all-gather.11.cloned.1.call-start = ((), (), s32[]{:S(2)}) async-start(), calls=%async_computation.14 | async-start | bytes 2162688 | tf_op jit(solution)/shard_map/all_gather | solution.py:394
  813.4 7.7 all-to-all-start.9
  (45 other events, 939.0 us)
Sparse Core Ops, SparseCore 0:
  11.4 67.8 all-gather.16
  82.8 63.3 all-gather.12
  149.7 63.0 all-gather.14
  308.2 94.0 all-reduce.15
  430.7 167.6 all-reduce.13
  600.6 17.9 reduce-scatter.5
  621.0 21.1 reduce-scatter.3
  644.4 45.5 all-gather.10
where the time goes:
time: 838 us; the launch traced here: 830 us
  waiting for transfers between devices  267 us (32%)
  blocking collectives  224 us (27%)
  matrix products  149 us (18%)
  other arithmetic  64.3 us (8%)
  local copies, waits for them, and re-layouts  57.8 us (7%)
  starting transfers between devices  50.4 us (6%)
  between operations  16.9 us (2%)
    unnamed x10, waiting for transfers between devices  220 us
    unnamed x1, blocking collectives  66.5 us
    all_gather x1, blocking collectives, shards(): lax.all_gather(output_weight.astype(jnp.bfloat16), ('fsdp', 'seq', 'tenso...  55.2 us
    all_gather x1, blocking collectives, shards(): lax.all_gather(vectors.astype(jnp.bfloat16), ('fsdp', 'seq', 'tensor'), a...  49 us
    dot_general x5, matrix products, orthogonalize(): gram_matrix = jnp.dot(current, current.T, precision=highest)  38.1 us
    dot_general x5, matrix products, orthogonalize(): jnp.dot(mixture, current, precision=highest)  36.5 us
    unnamed x111, local copies, waits for them, and re-layouts  22.4 us
    reduce_scatter x1, waiting for transfers between devices, shards(): lax.psum_scatter(combined.astype(jnp.bfloat16), 'tensor', scatter_dimensi...  21.4 us
  transfers between devices with their start and end apart: 17, of which 10 were waited for; matrix products, arithmetic and copies ran while one was open for 19% of the time, Pallas kernels for 0%

commit v1 on v0

v1 whole, which is shorter than its diff:
```python
import math

import jax
import jax.numpy as jnp
from jax import lax
from jax.experimental import pallas as pl
from jax.experimental.pallas import tpu as pltpu
from jax.sharding import PartitionSpec as P

D = 512
HEADS = 8
FF = 2048
ROT = 16
HD = 64
STEP = 10

norm_epsilon = 1e-05
masked_score = -1e30
newton_first = 3.4445
newton_second = -4.775
newton_third = 2.0315
beta_first = 0.9
beta_second = 0.95
adam_epsilon = 1e-08
vector_rate = 0.2
muon_rate = 0.25
muon_beta = 0.95
muon_decay = 0.01

BF = jnp.bfloat16
F32 = jnp.float32
MESH = pl.DeviceIdType.MESH
VMEM = pl.BlockSpec(memory_space=pltpu.VMEM)
SMEM = pl.BlockSpec(memory_space=pltpu.SMEM)
WIDTHS = (3 * D, D, FF, FF)


def shape(dims, dtype):
    return jax.ShapeDtypeStruct(dims, dtype)


class Place:
    def __init__(self):
        self.z = lax.axis_index("fsdp")
        seq = lax.axis_index("seq")
        self.t = lax.axis_index("tensor")
        self.x = lax.div(seq, 2)
        self.c = lax.rem(seq, 2)
        self.seq = seq
        self.g = 4 * self.c + self.t
        self.b = 4 * self.z + self.x
        self.d = 1 - 2 * self.c

    def at(self, z=None, x=None, c=None, t=None):
        z = self.z if z is None else z
        x = self.x if x is None else x
        c = self.c if c is None else c
        t = self.t if t is None else t
        return (z, 2 * x + c, t)

    def member(self, g):
        return self.at(c=lax.div(g, 4), t=lax.rem(g, 4))

    def sibling(self):
        return self.at(c=1 - self.c)

    def octet(self):
        return [self.member(lax.rem(self.g + k, 8)) for k in range(1, 8)]

    def row_x(self):
        return [self.at(x=lax.rem(self.x + k, 4)) for k in range(1, 4)]

    def row_z(self):
        return [self.at(z=lax.rem(self.z + k, 4)) for k in range(1, 4)]

    def row_t(self):
        return [self.at(t=lax.rem(self.t + k, 4)) for k in range(1, 4)]


def ring(index, step):
    return lax.rem(index + step + 4, 4)


def greet(partners):
    barrier = pltpu.get_barrier_semaphore()
    for partner in partners:
        pl.semaphore_signal(barrier, inc=1, device_id=partner, device_id_type=MESH)
    pl.semaphore_wait(barrier, len(partners))


class Wire:
    def __init__(self, send, recv):
        self.send = send
        self.recv = recv
        self.count = 0
        self.open = []

    def make(self, src, dst, device):
        index = self.count
        self.count += 1
        return pltpu.make_async_remote_copy(
            src_ref=src,
            dst_ref=dst,
            send_sem=self.send.at[index],
            recv_sem=self.recv.at[index],
            device_id=device,
            device_id_type=MESH,
        )

    def push(self, src, dst, device):
        copy = self.make(src, dst, device)
        copy.start()
        self.open.append(copy)
        return copy

    def drain(self):
        for copy in self.open:
            copy.wait_send()


def arrive(copies):
    for copy in copies:
        copy.wait_recv()


def dot(left, right):
    return jnp.dot(left, right, preferred_element_type=F32)


def dot_cols(left, right):
    return lax.dot_general(left, right, (((1,), (1,)), ((), ())), preferred_element_type=F32)


def dot_rows(left, right):
    return lax.dot_general(left, right, (((0,), (0,)), ((), ())), preferred_element_type=F32)


def exchange_octet(wire, place, out_ref, in_ref):
    copies = []
    for k in range(1, 8):
        goal = lax.rem(place.g + k, 8)
        copies.append(wire.push(out_ref.at[goal], in_ref.at[place.g], place.member(goal)))
    return copies


def gather_x(wire, place, ref):
    block = ref.at[place.c, place.b]
    return [wire.push(block, block, partner) for partner in place.row_x()]


def gather_z(wire, place, ref):
    z, c, d = place.z, place.c, place.d

    def part(index):
        return ref.at[c, pl.ds(4 * index, 4)]

    ahead, behind = ring(z, d), ring(z, -d)
    swaps = []
    first = wire.push(part(z), part(z), place.at(z=ahead))
    second = wire.push(part(z), part(z), place.at(z=behind))
    swaps.append(wire.push(part(z), part(z), place.sibling()))
    first.wait_recv()
    third = wire.push(part(behind), part(behind), place.at(z=ahead))
    swaps.append(wire.push(part(behind), part(behind), place.sibling()))
    second.wait_recv()
    swaps.append(wire.push(part(ahead), part(ahead), place.sibling()))
    third.wait_recv()
    opposite = ring(z, 2)
    swaps.append(wire.push(part(opposite), part(opposite), place.sibling()))
    return swaps


def gather_kernel(
    x_ref, c_ref, joint, output, expand, reduce, v_ref,
    w_out, rows_x, rows_c, v_out,
    out_buf, in_buf, whole, v_in, v_x, send, recv,
):
    place = Place()
    wire = Wire(send, recv)
    t, c, z, d = place.t, place.c, place.z, place.d
    greet(place.octet() + place.row_x() + place.row_z())
    for k in range(4):
        out_buf[k, :, 0:128] = joint[:, 128 * k : 128 * k + 128]
        out_buf[k, :, 128:256] = joint[:, 512 + 128 * k : 640 + 128 * k]
        out_buf[k, :, 256:384] = joint[:, 1024 + 128 * k : 1152 + 128 * k]
        out_buf[k, :, 384:896] = output[...]
        out_buf[k, :, 896:1024] = jnp.zeros((4, 128), F32)
        out_buf[4 + k, :, 0:512] = expand[:, 512 * k : 512 * k + 512]
        out_buf[4 + k, :, 512:1024] = reduce[:, 512 * k : 512 * k + 512]
    octet = exchange_octet(wire, place, out_buf, in_buf)
    for k, partner in enumerate(place.octet()):
        octet.append(wire.push(v_ref, v_in.at[place.g], partner))
    ahead, behind = ring(t, d), ring(t, -d)
    first, second = [], []
    for source, rows in ((x_ref, rows_x), (c_ref, rows_c)):
        first.append(wire.push(source, rows.at[t], place.at(t=ahead)))
        second.append(wire.push(source, rows.at[t], place.at(t=behind)))
        rows[t] = source[...]
    in_buf[place.g] = out_buf[place.g]
    v_in[place.g] = v_ref[...]
    arrive(octet)
    for k in range(8):
        whole[4 * k : 4 * k + 4, :] = in_buf[k]

    @pl.when(c == 0)
    def _():
        keys, values = whole[:, 128:256], whole[:, 256:384]
        low = lax.broadcasted_iota(jnp.int32, (32, 128), 1) < 64
        whole[:, 128:256] = jnp.where(low, keys, pltpu.roll(values, 64, 1))
        whole[:, 256:384] = jnp.where(low, pltpu.roll(keys, 64, 1), values)

    w_out[c, place.b] = whole[...].astype(BF)
    total = v_in[0]
    for k in range(1, 8):
        total = total + v_in[k]
    v_x[place.x] = total
    along = gather_x(wire, place, w_out)
    for partner in place.row_x():
        along.append(wire.push(v_x.at[place.x], v_x.at[place.x], partner))
    arrive(along)
    v_out[z] = (v_x[0] + v_x[1]) + (v_x[2] + v_x[3])
    spread = [wire.push(v_out.at[z], v_out.at[z], partner) for partner in place.row_z()]
    arrive(first)
    third = []
    for rows in (rows_x, rows_c):
        third.append(wire.push(rows.at[behind], rows.at[behind], place.at(t=ahead)))
    swaps = gather_z(wire, place, w_out)
    arrive(second)
    arrive(third)
    arrive(spread)
    arrive(swaps)
    wire.drain()


def gather_stage(block_input, cotangent, joint, output, expand, reduce, vec):
    return pl.pallas_call(
        gather_kernel,
        out_shape=(
            shape((2, 16, 32, 1024), BF),
            shape((4, 128, D), BF),
            shape((4, 128, D), BF),
            shape((4, 16, 128), F32),
        ),
        in_specs=[VMEM] * 7,
        out_specs=(VMEM,) * 4,
        scratch_shapes=[
            pltpu.VMEM((8, 4, 1024), F32),
            pltpu.VMEM((8, 4, 1024), F32),
            pltpu.VMEM((32, 1024), F32),
            pltpu.VMEM((8, 16, 128), F32),
            pltpu.VMEM((4, 16, 128), F32),
            pltpu.SemaphoreType.DMA((40,)),
            pltpu.SemaphoreType.DMA((40,)),
        ],
        compiler_params=pltpu.CompilerParams(
            collective_id=1, has_side_effects=True, vmem_limit_bytes=24 << 20
        ),
        name="gather",
    )(block_input, cotangent, joint, output, expand, reduce, vec)


def turn(values, cosine, sine, sign):
    lane = lax.broadcasted_iota(jnp.int32, values.shape, 1)
    lane = lax.rem(lane, 64)
    up = pltpu.roll(values, 120, 1)
    down = pltpu.roll(values, 8, 1)
    crossed = jnp.where(lane < 8, -up, down)
    return values * cosine + crossed * (sine * sign)


def vec_row(v_ref, row):
    return jnp.concatenate([v_ref[k, row : row + 1, :] for k in range(4)], axis=1)


def normalise(rows):
    wide = rows.astype(F32)
    centred = wide - jnp.mean(wide, axis=-1, keepdims=True)
    variance = jnp.mean(centred * centred, axis=-1, keepdims=True)
    rate = lax.rsqrt(variance + norm_epsilon)
    return centred * rate, rate


def project_kernel(
    rows_x, rows_c, w, v, cos, sin,
    normed, qo, kv, feed, row_grad, expand_grad, reduce_grad, hidden_sum,
    q_buf, kv_buf, hidden, pre, send, recv,
):
    place = Place()
    wire = Wire(send, recv)
    x, c, t, d = place.x, place.c, place.t, place.d
    partners = []
    for k in range(1, 8):
        other = lax.rem(place.seq + k, 8)
        partners.append((place.z, other, t))
    greet(partners)
    gain, shift = vec_row(v, 0), vec_row(v, 1)
    q_bias, k_bias, v_bias = v[t, 2:3, :], v[t, 3:4, :], v[t, 4:5, :]
    low_row = lax.broadcasted_iota(jnp.int32, (1, 128), 1) < 64
    pair_bias = (
        jnp.where(low_row, k_bias, pltpu.roll(v_bias, 64, 1)),
        jnp.where(low_row, pltpu.roll(k_bias, 64, 1), v_bias),
    )
    low = lax.broadcasted_iota(jnp.int32, (128, 128), 1) < 64

    def project(i, _):
        normal, _rate = normalise(rows_x[i])
        part = (normal * gain + shift).astype(BF)
        normed[i] = part
        raw = dot(part, w[0, :, :, 0:384].reshape(512, 384))
        out_rows = w[0, pl.ds(4 * t, 4), :, 384:896].reshape(128, 512)
        grad = dot_cols(rows_c[i], out_rows)
        cosine, sine = cos[i], sin[i]
        query = turn(raw[:, 0:128] + q_bias, cosine, sine, 1.0)
        q_buf[0, i] = jnp.where(low, query, pltpu.roll(grad, 64, 1)).astype(BF)
        q_buf[1, i] = jnp.where(low, pltpu.roll(query, 64, 1), grad).astype(BF)
        key_cos = jnp.where(low, cosine, 1.0)
        key_sin = jnp.where(low, sine, 0.0)
        for h in range(2):
            pair = raw[:, 128 + 128 * h : 256 + 128 * h] + pair_bias[h]
            kv_buf[h, i] = turn(pair, key_cos, key_sin, 1.0).astype(BF)
        return 0

    lax.fori_loop(0, 4, project, 0)
    own = place.seq
    swap = wire.push(kv_buf.at[1 - c], kv.at[own], place.sibling())
    first_q = wire.make(q_buf.at[0], qo.at[1], place.at(x=3 - x, c=0))
    second_q = wire.make(q_buf.at[1], qo.at[1], place.at(x=3 - x, c=1))
    near_q = wire.make(q_buf.at[1], qo.at[0], place.at(c=1))

    @pl.when(c == 0)
    def _():
        near_q.start()
        qo[0] = q_buf[0]

    @pl.when(c == 1)
    def _():
        first_q.start()
        second_q.start()

    kv[own] = kv_buf[c]

    def feed_forward(i, sums):
        wide = dot(normed[i], w[1, :, :, 0:512].reshape(512, 512))
        bias = jnp.concatenate([v[k, pl.ds(7 + t, 1), :] for k in range(4)], axis=1)
        wide = wide + bias
        square = wide * wide
        curve = jnp.tanh(0.7978845608 * (wide + 0.044715 * (square * wide)))
        hidden[i] = (0.5 * wide * (1.0 + curve)).astype(BF)
        slope = 0.5 * (1.0 + curve) + (0.5 * 0.7978845608) * wide * (1.0 - curve * curve) * (
            1.0 + (3 * 0.044715) * square
        )
        back = dot(rows_c[i], w[1, :, :, 512:1024].reshape(512, 512))
        grad = (back * slope).astype(BF)
        pre[i] = grad
        return sums + jnp.sum(grad.astype(F32), axis=0, keepdims=True)

    hidden_sum[...] = lax.fori_loop(0, 4, feed_forward, jnp.zeros((1, 512), F32))
    swap.wait_recv()

    def pair(index):
        return kv.at[pl.ds(2 * index, 2)]

    ahead, behind = ring(x, d), ring(x, -d)
    first = wire.push(pair(x), pair(x), place.at(x=ahead))
    second = wire.push(pair(x), pair(x), place.at(x=behind))

    def feed_out(i, _):
        feed[i] = dot_cols(hidden[i], w[1, :, :, 512:1024].reshape(512, 512))
        row_grad[i] = dot_cols(pre[i], w[1, :, :, 0:512].reshape(512, 512))
        return 0

    lax.fori_loop(0, 4, feed_out, 0)
    first.wait_recv()
    third = wire.push(pair(behind), pair(behind), place.at(x=ahead))
    for j in range(4):
        lanes = slice(128 * j, 128 * j + 128)
        reduce_grad[j] = dot_rows(
            rows_c[:, :, lanes].reshape(512, 128), hidden[...].reshape(512, 512)
        ).astype(BF)
        expand_grad[j] = dot_rows(
            normed[:, :, lanes].reshape(512, 128), pre[...].reshape(512, 512)
        ).astype(BF)
    second.wait_recv()
    third.wait_recv()

    @pl.when(c == 0)
    def _():
        near_q.wait_send()
        first_q.wait_recv()

    @pl.when(c == 1)
    def _():
        first_q.wait_send()
        second_q.wait_send()
        near_q.wait_recv()
        second_q.wait_recv()

    wire.drain()


def project_stage(rows_x, rows_c, w, v, cos, sin):
    return pl.pallas_call(
        project_kernel,
        out_shape=(
            shape((4, 128, D), BF),
            shape((2, 4, 128, 128), BF),
            shape((8, 4, 128, 128), BF),
            shape((4, 128, D), F32),
            shape((4, 128, D), F32),
            shape((4, 128, D), BF),
            shape((4, 128, D), BF),
            shape((1, 512), F32),
        ),
        in_specs=[VMEM] * 6,
        out_specs=(VMEM,) * 8,
        scratch_shapes=[
            pltpu.VMEM((2, 4, 128, 128), BF),
            pltpu.VMEM((2, 4, 128, 128), BF),
            pltpu.VMEM((4, 128, D), BF),
            pltpu.VMEM((4, 128, D), BF),
            pltpu.SemaphoreType.DMA((8,)),
            pltpu.SemaphoreType.DMA((8,)),
        ],
        compiler_params=pltpu.CompilerParams(
            collective_id=2, has_side_effects=True, vmem_limit_bytes=32 << 20
        ),
        name="project",
    )(rows_x, rows_c, w, v, cos, sin)


def attention_kernel(lengths, qo, kv, od, dkv, turned, scores, grads, sums):
    x = lax.div(lax.axis_index("seq"), 2)
    low = lax.broadcasted_iota(jnp.int32, (512, 128), 1) < 64
    sums[...] = jnp.zeros_like(sums)
    for k in range(8):
        turned[k] = kv[k].T

    for slot in range(2):
        chunk = 2 * x if slot == 0 else 7 - 2 * x
        packed = qo[slot]
        query = jnp.where(low, packed.astype(F32) * (HD ** -0.5), 0.0).astype(BF)
        out_grad = jnp.where(low, 0.0, packed.astype(F32)).astype(BF)
        index = 512 * chunk + lax.broadcasted_iota(jnp.int32, (1, 512), 1)
        begin = jnp.zeros((1, 512), jnp.int32)
        finish = 0
        for j in range(4):
            finish = finish + lengths[0, j]
            begin = jnp.where(index >= finish, finish, begin)

        def first(k, top):
            raw = dot_cols(kv[k], query)
            key = 512 * k + lax.broadcasted_iota(jnp.int32, (512, 512), 0)
            raw = jnp.where((key <= index) & (key >= begin), raw, masked_score)
            scores[k] = raw
            return jnp.maximum(top, jnp.max(raw, axis=0, keepdims=True))

        top = lax.fori_loop(0, chunk + 1, first, jnp.full((1, 512), masked_score, F32))

        def second(k, total):
            power = jnp.exp(scores[k] - top)
            scores[k] = power
            return total + jnp.sum(power, axis=0, keepdims=True)

        total = lax.fori_loop(0, chunk + 1, second, jnp.zeros((1, 512), F32))
        inverse = 1.0 / total

        def third(k, carry):
            centre, out = carry
            prob = scores[k] * inverse
            scores[k] = prob
            grad = dot_cols(kv[k], out_grad)
            grads[k] = grad
            prob_low = prob.astype(BF)
            out = out + dot(turned[k, 64:128, :], prob_low)
            sums[k] += dot(prob_low, out_grad)
            return centre + jnp.sum(prob * grad, axis=0, keepdims=True), out

        centre, out = lax.fori_loop(
            0, chunk + 1, third, (jnp.zeros((1, 512), F32), jnp.zeros((64, 512), F32))
        )

        def fourth(k, back):
            grad_low = (scores[k] * (grads[k] - centre)).astype(BF)
            sums[k] += dot(grad_low, query)
            return back + dot(turned[k, 0:64, :], grad_low)

        back = lax.fori_loop(0, chunk + 1, fourth, jnp.zeros((64, 512), F32))
        both = jnp.concatenate([out, back * (HD ** -0.5)], axis=0)
        od[slot] = both.T.astype(BF)
    dkv[...] = sums[...].astype(BF)


def attention_stage(lengths, qo, kv):
    return pl.pallas_call(
        attention_kernel,
        out_shape=(shape((2, 512, 128), BF), shape((8, 512, 128), BF)),
        in_specs=[SMEM, VMEM, VMEM],
        out_specs=(VMEM,) * 2,
        scratch_shapes=[
            pltpu.VMEM((8, 128, 512), BF),
            pltpu.VMEM((8, 512, 512), F32),
            pltpu.VMEM((8, 512, 512), F32),
            pltpu.VMEM((8, 512, 128), F32),
        ],
        compiler_params=pltpu.CompilerParams(vmem_limit_bytes=44 << 20),
        name="attention",
    )(lengths, qo, kv)


def backward_kernel(
    od, dkv, normed, rows_x, rows_c, w, v, cos, sin, feed, row_grad, expand_grad, reduce_grad,
    hidden_sum,
    grads, out_part, back_part, vec_part,
    od_in, near, mid, far, keep, give, took, pair_out, joint_out, out_cols, out_in, send, recv,
):
    place = Place()
    wire = Wire(send, recv)
    x, c, t, d = place.x, place.c, place.t, place.d
    partners = []
    for k in range(1, 8):
        partners.append((place.z, lax.rem(place.seq + k, 8), t))
    greet(partners + place.row_t())
    ahead, behind, opposite = ring(x, d), ring(x, -d), ring(x, 2)

    def pair(index):
        return dkv.at[pl.ds(2 * index, 2)]

    first = wire.push(pair(opposite), near, place.at(x=ahead))
    second = wire.push(pair(behind), far, place.at(x=behind))
    near_o = wire.make(od.at[0], od_in.at[1], place.at(c=0))
    first_o = wire.make(od.at[1], od_in.at[0], place.at(x=3 - x, c=1))
    second_o = wire.make(od.at[1], od_in.at[1], place.at(x=3 - x, c=1))

    @pl.when(c == 0)
    def _():
        first_o.start()
        od_in[0] = od[0]

    @pl.when(c == 1)
    def _():
        near_o.start()
        second_o.start()

    first.wait_recv()
    mid[...] = (near[...].astype(F32) + dkv[pl.ds(2 * ahead, 2)].astype(F32)).astype(BF)
    third = wire.push(mid, keep, place.at(x=ahead))

    @pl.when(c == 0)
    def _():
        first_o.wait_send()
        near_o.wait_recv()

    @pl.when(c == 1)
    def _():
        near_o.wait_send()
        second_o.wait_send()
        first_o.wait_recv()
        second_o.wait_recv()

    low = lax.broadcasted_iota(jnp.int32, (128, 128), 1) < 64
    for i in range(4):
        rows = pl.ds(128 * i, 128)
        left = od_in[0, rows, :].astype(F32)
        right = od_in[1, rows, :].astype(F32)
        joined = jnp.where(low, left, pltpu.roll(right, 64, 1)).astype(BF)
        pair_out[rows, :] = joined
        back = jnp.where(low, pltpu.roll(left, 64, 1), right)
        joint_out[rows, 0:128] = turn(back, cos[i], sin[i], -1.0).astype(BF)
        out_rows = w[0, pl.ds(4 * t, 4), :, 384:896].reshape(128, 512)
        out_part[i] = (feed[i] + dot(joined, out_rows)).astype(BF)
    for j in range(4):
        part = rows_c[:, :, 128 * j : 128 * j + 128].reshape(512, 128)
        out_cols[j] = dot_rows(pair_out[...], part).astype(BF)
    out_in[t] = out_cols[t]
    trade = []
    for k in range(1, 4):
        goal = lax.rem(t + k, 4)
        trade.append(wire.push(out_cols.at[goal], out_in.at[t], place.at(t=goal)))
    for j in range(4):
        grads[1, 4 * j : 4 * j + 4, :, 0:512] = expand_grad[j].reshape(4, 32, 512)
        grads[1, 4 * j : 4 * j + 4, :, 512:768] = reduce_grad[j, :, 256:512].reshape(4, 32, 256)
        grads[0, 4 * j : 4 * j + 4, :, 512:768] = reduce_grad[j, :, 0:256].reshape(4, 32, 256)
    second.wait_recv()
    third.wait_recv()
    other = 1 - c
    give[...] = (
        dkv[2 * x + other].astype(F32) + far[other].astype(F32) + keep[other].astype(F32)
    ).astype(BF)
    swap = wire.push(give, took.at[c], place.sibling())
    took[c] = (
        dkv[2 * x + c].astype(F32) + far[c].astype(F32) + keep[c].astype(F32)
    ).astype(BF)
    swap.wait_recv()
    for h in range(2):
        for i in range(4):
            rows = pl.ds(128 * i, 128)
            part = took[h, rows, :].astype(F32)
            key_cos = jnp.where(low, cos[i], 1.0)
            key_sin = jnp.where(low, sin[i], 0.0)
            joint_out[rows, 128 + 128 * h : 256 + 128 * h] = turn(
                part, key_cos, key_sin, -1.0
            ).astype(BF)
    for j in range(4):
        part = normed[:, :, 128 * j : 128 * j + 128].reshape(512, 128)
        grads[0, 4 * j : 4 * j + 4, :, 0:384] = (
            dot_rows(part, joint_out[...]).astype(BF).reshape(4, 32, 384)
        )
    vec_part[...] = jnp.zeros_like(vec_part)
    shift_sum = jnp.zeros((1, 512), F32)
    gain_sum = jnp.zeros((1, 512), F32)
    for i in range(4):
        rows = pl.ds(128 * i, 128)
        part = row_grad[i] + dot_cols(
            joint_out[rows, :], w[0, :, :, 0:384].reshape(512, 384)
        )
        back_part[i] = part.astype(BF)
        normal, _rate = normalise(rows_x[i])
        shift_sum = shift_sum + jnp.sum(part, axis=0, keepdims=True)
        gain_sum = gain_sum + jnp.sum(part * normal, axis=0, keepdims=True)
    out_sum = jnp.sum(rows_c[t].astype(F32), axis=0, keepdims=True)
    joint_sum = jnp.sum(joint_out[...].astype(F32), axis=0, keepdims=True)
    one, two = joint_sum[:, 128:256], joint_sum[:, 256:384]
    low_row = lax.broadcasted_iota(jnp.int32, (1, 128), 1) < 64
    for k in range(4):
        lanes = slice(128 * k, 128 * k + 128)
        vec_part[k, 0:1, :] = gain_sum[:, lanes]
        vec_part[k, 1:2, :] = shift_sum[:, lanes]
        vec_part[k, 5:6, :] = out_sum[:, lanes]
        vec_part[k, 6:7, :] = out_sum[:, lanes]
        vec_part[k, pl.ds(7 + t, 1), :] = hidden_sum[:, lanes]
    vec_part[t, 2:3, :] = joint_sum[:, 0:128]
    vec_part[t, 3:4, :] = jnp.where(low_row, one, pltpu.roll(two, 64, 1))
    vec_part[t, 4:5, :] = jnp.where(low_row, pltpu.roll(one, 64, 1), two)
    arrive(trade)
    for j in range(4):
        grads[0, 4 * j : 4 * j + 4, :, 384:512] = out_in[j].reshape(4, 32, 128)
    wire.drain()


def backward_stage(*arrays):
    return pl.pallas_call(
        backward_kernel,
        out_shape=(
            shape((2, 16, 32, 768), BF),
            shape((4, 128, D), BF),
            shape((4, 128, D), BF),
            shape((4, 16, 128), F32),
        ),
        in_specs=[VMEM] * 14,
        out_specs=(VMEM,) * 4,
        scratch_shapes=[
            pltpu.VMEM((2, 512, 128), BF),
            pltpu.VMEM((2, 512, 128), BF),
            pltpu.VMEM((2, 512, 128), BF),
            pltpu.VMEM((2, 512, 128), BF),
            pltpu.VMEM((2, 512, 128), BF),
            pltpu.VMEM((512, 128), BF),
            pltpu.VMEM((2, 512, 128), BF),
            pltpu.VMEM((512, 128), BF),
            pltpu.VMEM((512, 384), BF),
            pltpu.VMEM((4, 128, 128), BF),
            pltpu.VMEM((4, 128, 128), BF),
            pltpu.SemaphoreType.DMA((12,)),
            pltpu.SemaphoreType.DMA((12,)),
        ],
        compiler_params=pltpu.CompilerParams(
            collective_id=3, has_side_effects=True, vmem_limit_bytes=40 << 20
        ),
        name="backward",
    )(*arrays)


def reduce_kernel(
    grads, out_part, back_part, vec_part, x_ref, c_ref, v, m_joint, m_output, m_expand, m_reduce,
    g_joint, g_output, g_expand, g_reduce, n_joint, n_output, n_expand, n_reduce,
    block_output, input_grad, vec_sum, moments,
    core_in, chip, near, mid, far, keep, x_out, x_in, out_buf, in_buf, out_in, back_in,
    v_core, v_acc, v_z, v_x, v_t, send, recv,
):
    place = Place()
    wire = Wire(send, recv)
    z, x, c, t, d = place.z, place.x, place.c, place.t, place.d
    greet(place.octet() + place.row_x() + place.row_z())
    sibling = place.sibling()
    ahead, behind, opposite = ring(z, d), ring(z, -d), ring(z, 2)

    def part(ref, index):
        return ref.at[pl.ds(4 * index, 4)]

    handed = []
    for index in (opposite, ahead, behind, z):
        handed.append(
            wire.push(grads.at[1 - c, pl.ds(4 * index, 4)], part(core_in, index), sibling)
        )
    v_swap = wire.push(vec_part, v_core, sibling)
    swaps = []
    for k in range(1, 4):
        goal = lax.rem(t + k, 4)
        swaps.append(wire.push(back_part.at[goal], back_in.at[k - 1], place.at(t=goal)))
        swaps.append(wire.push(out_part.at[goal], out_in.at[k - 1], place.at(t=goal)))

    def chip_sum(index):
        rows = pl.ds(4 * index, 4)
        return grads[c, rows].astype(F32) + core_in[rows].astype(F32)

    handed[0].wait_recv()
    chip[0] = chip_sum(opposite).astype(BF)
    first = wire.push(chip.at[0], near, place.at(z=ahead))
    handed[1].wait_recv()
    chip[1] = chip_sum(behind).astype(BF)
    second = wire.push(chip.at[1], far, place.at(z=behind))
    v_swap.wait_recv()
    v_acc[0] = vec_part[...] + v_core[...]
    v_first = [wire.push(v_acc.at[0], v_z.at[k], p) for k, p in enumerate(place.row_z())]
    handed[2].wait_recv()
    first.wait_recv()
    mid[...] = (near[...].astype(F32) + chip_sum(ahead)).astype(BF)
    third = wire.push(mid, keep, place.at(z=ahead))
    arrive(v_first)
    v_acc[1] = (v_acc[0] + v_z[0]) + (v_z[1] + v_z[2])
    v_second = [wire.push(v_acc.at[1], v_x.at[k], p) for k, p in enumerate(place.row_x())]
    handed[3].wait_recv()
    second.wait_recv()
    partial = chip_sum(z) + far[...].astype(F32)
    third.wait_recv()
    x_sum = partial + keep[...].astype(F32)
    x_out[...] = x_sum.astype(BF)
    along = []
    for k in range(1, 4):
        goal = lax.rem(x + k, 4)
        along.append(wire.push(x_out.at[goal], x_in.at[k - 1], place.at(x=goal)))
    arrive(v_second)
    v_acc[2] = (v_acc[1] + v_x[0]) + (v_x[1] + v_x[2])
    v_third = [wire.push(v_acc.at[2], v_t.at[k], p) for k, p in enumerate(place.row_t())]
    arrive(along)
    own = x_out[x].astype(F32)
    for k in range(3):
        own = own + x_in[k].astype(F32)
    for k in range(8):
        out_buf[k] = own[4 * k : 4 * k + 4, :]
    octet = exchange_octet(wire, place, out_buf, in_buf)
    in_buf[place.g] = out_buf[place.g]

    arrive(swaps)
    wide = x_ref[...].astype(F32)
    feed = out_part[t].astype(F32)
    back = back_part[t].astype(F32)
    for k in range(3):
        feed = feed + out_in[k].astype(F32)
        back = back + back_in[k].astype(F32)
    block_output[...] = (wide + feed + vec_row(v, 5) + vec_row(v, 6)).astype(BF)
    normal, rate = normalise(x_ref[...])
    scaled = back * vec_row(v, 0)
    mean_one = jnp.mean(scaled, axis=-1, keepdims=True)
    mean_two = jnp.mean(scaled * normal, axis=-1, keepdims=True)
    input_grad[...] = c_ref[...].astype(F32) + rate * (scaled - mean_one - normal * mean_two)

    arrive(octet)
    for k in range(4):
        lanes = slice(128 * k, 128 * k + 128)
        first_kind, second_kind = in_buf[k], in_buf[4 + k]
        g_joint[:, lanes] = first_kind[:, 0:128]
        one, two = first_kind[:, 128:256], first_kind[:, 256:384]
        g_joint[:, 512 + 128 * k : 640 + 128 * k] = jnp.concatenate(
            [one[:, 0:64], two[:, 0:64]], axis=1
        )
        g_joint[:, 1024 + 128 * k : 1152 + 128 * k] = jnp.concatenate(
            [one[:, 64:128], two[:, 64:128]], axis=1
        )
        g_output[:, lanes] = first_kind[:, 384:512]
        g_expand[:, 512 * k : 512 * k + 512] = second_kind[:, 0:512]
        g_reduce[:, 512 * k : 512 * k + 256] = first_kind[:, 512:768]
        g_reduce[:, 512 * k + 256 : 512 * k + 512] = second_kind[:, 512:768]
    moments[...] = jnp.zeros_like(moments)
    for k, (old, grad, new) in enumerate(
        (
            (m_joint, g_joint, n_joint),
            (m_output, g_output, n_output),
            (m_expand, g_expand, n_expand),
            (m_reduce, g_reduce, n_reduce),
        )
    ):
        value = muon_beta * old[...] + grad[...]
        new[...] = value
        width = min(WIDTHS[k], 1024)
        moments[k, :, 0:width] = value[:, 0:width]
        if WIDTHS[k] > 1024:
            moments[4 + k, :, 0 : WIDTHS[k] - 1024] = value[:, 1024:]
    arrive(v_third)
    vec_sum[...] = (v_acc[2] + v_t[0]) + (v_t[1] + v_t[2])
    wire.drain()


def reduce_stage(*arrays):
    narrow = [shape((4, width), F32) for width in WIDTHS]
    block = pltpu.VMEM((4, 32, 768), BF)
    return pl.pallas_call(
        reduce_kernel,
        out_shape=(
            *narrow,
            *narrow,
            shape((128, D), BF),
            shape((128, D), F32),
            shape((4, 16, 128), F32),
            shape((8, 4, 1024), F32),
        ),
        in_specs=[VMEM] * 11,
        out_specs=(VMEM,) * 12,
        scratch_shapes=[
            pltpu.VMEM((16, 32, 768), BF),
            pltpu.VMEM((2, 4, 32, 768), BF),
            block,
            block,
            block,
            block,
            block,
            pltpu.VMEM((3, 32, 768), BF),
            pltpu.VMEM((8, 4, 768), F32),
            pltpu.VMEM((8, 4, 768), F32),
            pltpu.VMEM((3, 128, D), BF),
            pltpu.VMEM((3, 128, D), BF),
            pltpu.VMEM((4, 16, 128), F32),
            pltpu.VMEM((3, 4, 16, 128), F32),
            pltpu.VMEM((3, 4, 16, 128), F32),
            pltpu.VMEM((3, 4, 16, 128), F32),
            pltpu.VMEM((3, 4, 16, 128), F32),
            pltpu.SemaphoreType.DMA((40,)),
            pltpu.SemaphoreType.DMA((40,)),
        ],
        compiler_params=pltpu.CompilerParams(
            collective_id=4, has_side_effects=True, vmem_limit_bytes=32 << 20
        ),
        name="reduce",
    )(*arrays)


def halves(values):
    high = values.astype(BF)
    return high, (values - high.astype(F32)).astype(BF)


def muon_kernel(
    moments, w_joint, w_output, w_expand, w_reduce,
    u_joint, u_output, u_expand, u_reduce,
    in_buf, whole, momentum, gram, gram_h, gram_l, poly_h, poly_l, temp_h, temp_l, out_buf, back_buf,
    send, recv,
):
    place = Place()
    wire = Wire(send, recv)
    c = place.c
    greet(place.octet() + place.row_x() + place.row_z())
    octet = exchange_octet(wire, place, moments, in_buf)
    in_buf[place.g] = moments[place.g]
    arrive(octet)
    for k in range(8):
        whole[4 * k : 4 * k + 4, :] = in_buf[k]
    momentum[c, place.b] = whole[...].astype(BF)
    arrive(gather_x(wire, place, momentum))
    arrive(gather_z(wire, place, momentum))

    def flat(ref):
        return ref[...].reshape(512, 512)

    def block(ref, i):
        return ref[pl.ds(4 * i, 4)].reshape(128, 512)

    def fill(i, total):
        rows = pl.ds(4 * i, 4)
        value = jnp.zeros((128, 512), F32)
        for k in range(2):
            value = value + dot_cols(
                momentum[k, rows].reshape(128, 1024), momentum[k].reshape(512, 1024)
            )
        gram[rows] = value.reshape(4, 32, 512)
        row = 128 * i + lax.broadcasted_iota(jnp.int32, (128, 512), 0)
        column = lax.broadcasted_iota(jnp.int32, (128, 512), 1)
        return total + jnp.sum(jnp.where(row == column, value, 0.0), keepdims=True)

    total = lax.fori_loop(0, 4, fill, jnp.zeros((1, 1), F32))
    scale = 1.0 / (jnp.sqrt(total) + 1e-07)

    def prepare(i, _):
        rows = pl.ds(4 * i, 4)
        value = block(gram, i) * (scale * scale)
        gram[rows] = value.reshape(4, 32, 512)
        high, small = halves(value)
        gram_h[rows] = high.reshape(4, 32, 512)
        gram_l[rows] = small.reshape(4, 32, 512)
        return 0

    lax.fori_loop(0, 4, prepare, 0)

    def product(left_h, left_l, right_h, right_l):
        return dot(left_h, right_h) + (dot(left_h, right_l) + dot(left_l, right_h))

    def polynomial(i, _):
        rows = pl.ds(4 * i, 4)
        square = product(block(gram_h, i), block(gram_l, i), flat(gram_h), flat(gram_l))
        row = 128 * i + lax.broadcasted_iota(jnp.int32, (128, 512), 0)
        column = lax.broadcasted_iota(jnp.int32, (128, 512), 1)
        value = (
            jnp.where(row == column, newton_first, 0.0)
            + newton_second * block(gram, i)
            + newton_third * square
        )
        high, small = halves(value)
        poly_h[rows] = high.reshape(4, 32, 512)
        poly_l[rows] = small.reshape(4, 32, 512)
        return 0

    def inner(i, _):
        rows = pl.ds(4 * i, 4)
        value = product(block(gram_h, i), block(gram_l, i), flat(poly_h), flat(poly_l))
        high, small = halves(value)
        temp_h[rows] = high.reshape(4, 32, 512)
        temp_l[rows] = small.reshape(4, 32, 512)
        return 0

    def outer(i, _):
        rows = pl.ds(4 * i, 4)
        value = product(block(temp_h, i), block(temp_l, i), flat(poly_h), flat(poly_l))
        gram[rows] = value.reshape(4, 32, 512)
        high, small = halves(value)
        gram_h[rows] = high.reshape(4, 32, 512)
        gram_l[rows] = small.reshape(4, 32, 512)
        return 0

    def times(left, right_h, right_l):
        high, small = halves(left)
        return product(high, small, flat(right_h), flat(right_l))

    own = None
    for sweep in range(4):
        lax.fori_loop(0, 4, polynomial, 0)
        if sweep == 0:
            own = poly_h[place.b].astype(F32) + poly_l[place.b].astype(F32)
        else:
            own = times(own, poly_h, poly_l)
        if sweep < 3:
            lax.fori_loop(0, 4, inner, 0)
            lax.fori_loop(0, 4, outer, 0)

    def last_gram(left):
        left = times(left, gram_h, gram_l)
        left = times(left, poly_h, poly_l)
        return times(left, poly_h, poly_l)

    once = last_gram(own)
    own = newton_first * own + newton_second * once + newton_third * last_gram(once)
    high, small = halves(own * scale)
    columns = momentum[c].reshape(512, 1024)
    result = dot(high, columns) + dot(small, columns)
    for k in range(8):
        out_buf[k] = result[4 * k : 4 * k + 4, :]
    octet = exchange_octet(wire, place, out_buf, back_buf)
    back_buf[place.g] = out_buf[place.g]
    arrive(octet)
    for k, (old, new) in enumerate(
        ((w_joint, u_joint), (w_output, u_output), (w_expand, u_expand), (w_reduce, u_reduce))
    ):
        factor = muon_rate * 0.2 * math.sqrt(max(D, WIDTHS[k]))
        for half in range(2):
            start = 1024 * half
            stop = min(WIDTHS[k], start + 1024)
            if stop > start:
                new[:, start:stop] = (
                    old[:, start:stop] * (1.0 - muon_rate * muon_decay)
                    - factor * back_buf[4 * half + k, :, 0 : stop - start]
                )
    wire.drain()


def muon_stage(*arrays):
    square = pltpu.VMEM((16, 32, 512), BF)
    return pl.pallas_call(
        muon_kernel,
        out_shape=tuple(shape((4, width), F32) for width in WIDTHS),
        in_specs=[VMEM] * 5,
        out_specs=(VMEM,) * 4,
        scratch_shapes=[
            pltpu.VMEM((8, 4, 1024), F32),
            pltpu.VMEM((32, 1024), F32),
            pltpu.VMEM((2, 16, 32, 1024), BF),
            pltpu.VMEM((16, 32, 512), F32),
            square,
            square,
            square,
            square,
            square,
            square,
            pltpu.VMEM((8, 4, 1024), F32),
            pltpu.VMEM((8, 4, 1024), F32),
            pltpu.SemaphoreType.DMA((32,)),
            pltpu.SemaphoreType.DMA((32,)),
        ],
        compiler_params=pltpu.CompilerParams(
            collective_id=5, has_side_effects=True, vmem_limit_bytes=32 << 20
        ),
        name="muon",
    )(*arrays)


def tables(lengths, seq):
    index = 512 * seq + jnp.arange(512, dtype=jnp.int32)
    finish = jnp.cumsum(lengths, dtype=jnp.int32)
    passed = index[:, None] >= finish[None, :]
    starts = jnp.sum(jnp.where(passed, lengths[None, :], 0), axis=1, dtype=jnp.int32)
    position = (index - starts).astype(F32)
    half = ROT // 2
    frequency = 10000.0 ** (-(jnp.arange(half, dtype=F32) * 2.0) / ROT)
    head = jnp.concatenate([frequency, frequency, jnp.zeros((HD - ROT,), F32)])
    angle = position[:, None] * jnp.concatenate([head, head])[None, :]
    return jnp.cos(angle).reshape(4, 128, 128), jnp.sin(angle).reshape(4, 128, 128)


def shards(
    block_input,
    cotangent,
    doc_lengths,
    joint_weight,
    output_weight,
    expand_weight,
    reduce_weight,
    joint_moment,
    output_moment,
    expand_moment,
    reduce_moment,
    vectors,
    first_moment,
    second_moment,
):
    z = lax.axis_index("fsdp")
    seq = lax.axis_index("seq")
    t = lax.axis_index("tensor")
    place = 16 * seq + 4 * t
    cos, sin = tables(doc_lengths[0], seq)
    vec = lax.dynamic_update_slice(
        jnp.zeros((16, 128), F32), vectors.astype(BF).astype(F32), (0, place)
    )
    w, rows_x, rows_c, v = gather_stage(
        block_input, cotangent, joint_weight, output_weight, expand_weight, reduce_weight, vec
    )
    normed, qo, kv, feed, row_grad, expand_grad, reduce_grad, hidden_sum = project_stage(
        rows_x, rows_c, w, v, cos, sin
    )
    od, dkv = attention_stage(doc_lengths, qo.reshape(2, 512, 128), kv.reshape(8, 512, 128))
    grads, out_part, back_part, vec_part = backward_stage(
        od, dkv, normed, rows_x, rows_c, w, v, cos, sin, feed, row_grad, expand_grad, reduce_grad,
        hidden_sum,
    )
    reduced = reduce_stage(
        grads, out_part, back_part, vec_part, block_input, cotangent, v,
        joint_moment, output_moment, expand_moment, reduce_moment,
    )
    gradients, momenta = reduced[0:4], reduced[4:8]
    block_output, input_grad, vec_sum, moments = reduced[8:]
    updated = muon_stage(moments, joint_weight, output_weight, expand_weight, reduce_weight)
    vector_grad = lax.dynamic_slice(vec_sum, (z, 0, place), (1, 11, 4)).reshape(11, 4)
    first_next = beta_first * first_moment + (1.0 - beta_first) * vector_grad
    second_next = beta_second * second_moment + (1.0 - beta_second) * vector_grad * vector_grad
    first_hat = first_next / (1.0 - beta_first**STEP)
    second_hat = second_next / (1.0 - beta_second**STEP)
    vector_next = vectors - vector_rate * first_hat / (jnp.sqrt(second_hat) + adam_epsilon)
    return (
        block_output,
        input_grad,
        *gradients,
        *momenta,
        *updated,
        vector_grad,
        second_next,
        vector_next,
    )


def solution(mesh):
    rows = P(("fsdp", "seq", "tensor"), None)
    columns = P(None, ("fsdp", "seq", "tensor"))
    return jax.shard_map(
        shards,
        mesh=mesh,
        in_specs=(rows, rows, P("fsdp", None)) + (rows,) * 8 + (columns,) * 3,
        out_specs=(rows,) * 14 + (columns,) * 3,
        check_vma=False,
    )
```

time: 838 us -> 184 us (0.22)
  waiting for transfers between devices: 267 us -> 0 us
  blocking collectives: 224 us -> 0 us
  Pallas kernels: 0 us -> 165 us
  matrix products: 149 us -> 0 us
  other arithmetic: 64.3 us -> 3.87 us
  starting transfers between devices: 50.4 us -> 0 us
  local copies, waits for them, and re-layouts: 57.8 us -> 14.6 us
  between operations: 16.9 us -> 0.94 us
    unnamed x10 -> x0, waiting for transfers between devices: 220 us -> none
    pallas_call x0 -> x6, Pallas kernels: none -> 165 us  [the longest x1 54.1 us: muon_stage(): pl.pallas_call(muon_kernel, out_shape=tuple((shape((4, width), F32) for w...]
    all_gather x6 -> x0, blocking collectives: 149 us -> none  [the longest x1 55.2 us: shards(): lax.all_gather(output_weight.astype(jnp.bfloat16), ('fsdp', 'seq', 'tenso...]
    dot_general x42 -> x0, matrix products: 149 us -> none  [the longest x5 38.1 us: orthogonalize(): gram_matrix = jnp.dot(current, current.T, precision=highest)]
    unnamed x1 -> x0, blocking collectives: 66.5 us -> none
    all_to_all x9 -> x0, starting transfers between devices: 50.1 us -> none  [the longest x1 10.4 us: shards(): lax.all_to_all(query_grads.reshape(query_count, heads_here, HD).astype(jn...]
    reduce_scatter x2 -> x0, waiting for transfers between devices: 25.7 us -> none  [the longest x1 21.4 us: shards(): lax.psum_scatter(combined.astype(jnp.bfloat16), 'tensor', scatter_dimensi...]
    convert_element_type x10 -> x3, other arithmetic: 24.2 us -> 0.71 us  [the longest x2 0.69 us: shards(): vectors.astype(BF).astype(F32)]
  transfers between devices with their start and end apart: 17 -> 0, of which waited for: 10 -> 0; matrix products, arithmetic and copies ran while one was open for 19% -> 0% of each run, Pallas kernels for 0% -> 0%
where the time goes in v1:
time: 184 us
  Pallas kernels  165 us (90%)
  local copies, waits for them, and re-layouts  14.6 us (8%)
  other arithmetic  3.87 us (2%)
    pallas_call x1, Pallas kernels, muon_stage(): pl.pallas_call(muon_kernel, out_shape=tuple((shape((4, width), F32) for w...  54.1 us
    pallas_call x1, Pallas kernels, gather_stage(): pl.pallas_call(gather_kernel, out_shape=(shape((2, 16, 32, 1024), BF), sh...  32.4 us
    pallas_call x1, Pallas kernels, reduce_stage(): pl.pallas_call(reduce_kernel, out_shape=(*narrow, *narrow, shape((128, D)...  24.4 us
    pallas_call x1, Pallas kernels, backward_stage(): pl.pallas_call(backward_kernel, out_shape=(shape((2, 16, 32, 768), BF), s...  19.9 us
    pallas_call x1, Pallas kernels, project_stage(): pl.pallas_call(project_kernel, out_shape=(shape((4, 128, D), BF), shape((...  19.3 us
    pallas_call x1, Pallas kernels, attention_stage(): pl.pallas_call(attention_kernel, out_shape=(shape((2, 512, 128), BF), sha...  14.4 us
    unnamed x56, local copies, waits for them, and re-layouts  13.5 us

profile of v1, /device:TPU:1, one launch (start us, length us, event | category | flops | bytes accessed | tf_op | source)
XLA Modules:
  0.0 183.9 jit_solution(11500918505911453151)
XLA Ops:
  0.7 0.8 reduce-window.8
  1.6 0.7 convert_element_type.13
  2.3 0.7 select_reduce_fusion
  3.1 0.7 dynamic_update_slice.3.v_ref
  3.9 1.0 multiply_sine_fusion
  4.9 0.9 copy-done
  5.8 0.9 copy-done.2
  6.7 0.8 copy-done.4
  7.4 0.8 copy-done.6
  8.2 0.7 copy-done.8
  8.9 0.7 copy-done.12
  9.6 32.4 %gather.1 = (bf16[2,16,32,1024]{3,2,1,0:T(8,128)(2,1)S(1)}, bf16[4,128,512]{2,1,0:T(8,128)(2,1)S(1)}, bf16[4,128,512]{2,1,0:T(8,128)(2,1)S(1)}, f32[4,16,128]{2,1,0:T(8,128)S(1)}) custom-call(bf16[128,512]{1,0:T(8,128)(2,1)S(1)} %copy-done, bf16[128,512]{1,0:T(8,128)(2,1)S(1)} %copy-done.2, f32[4,1536]{1,0:T(4,128)S(1)} %copy-done.8, ...), custom_call_target="tpu_custom_call" | custom-call | tf_op jit(solution)/shard_map/gather/pallas_call | solution.py:236
  42.0 19.3 %project.1 = (bf16[4,128,512]{2,1,0:T(8,128)(2,1)S(1)}, bf16[2,4,128,128]{3,2,1,0:T(8,128)(2,1)S(1)}, bf16[8,4,128,128]{3,2,1,0:T(8,128)(2,1)S(1)}, f32[4,128,51...) custom-call(bf16[4,128,512]{2,1,0:T(8,128)(2,1)S(1)} %get-tuple-elem, ...), custom_call_target="tpu_custom_call" | custom-call | tf_op jit(solution)/shard_map/project/pallas_call | solution.py:402
  61.4 14.4 %attention.1 = (bf16[2,512,128]{2,1,0:T(8,128)(2,1)S(1)}, bf16[8,512,128]{2,1,0:T(8,128)(2,1)S(1)}) custom-call(s32[1,4]{1,0:T(1,128)S(1)} %copy-done.16, bf16[2,512,128]{2,1,0:T(8,128)(2,1)S(1)} %bitcast.12, bf16[8,512,128]{2,1,0:T(8,128)(2,1)S(1)} %bitcast.11), custom_call_target="tpu_custom_call" | custom-call | tf_op jit(solution)/shard_map/attention/pallas_call | solution.py:494
  75.8 19.9 %backward.1 = (bf16[2,16,32,768]{3,2,1,0:T(8,128)(2,1)S(1)}, bf16[4,128,512]{2,1,0:T(8,128)(2,1)S(1)}, bf16[4,128,512]{2,1,0:T(8,128)(2,1)S(1)}, f32[4,16,128]{2,1,0:T(8,128)S(1)}) custom-call(bf16[2,512,128]{2,1,0:T(8,128)(2,1)S(1)} %get-tuple-element.57.od, bf16[8,512,128]{2,1,0:T(8,128)(2,1)S(1)} %get-tuple-element.58.dkv, ...), custom_call_target="tpu_custom_call" | custom-call | tf_op jit(solution)/shard_map/backward/pallas_call | solution.py:641
  95.9 24.4 %reduce.3 = (f32[4,1536]{1,0:T(4,128)S(1)}, f32[4,512]{1,0:T(4,128)S(1)}, f32[4,2048]{1,0:T(4,128)S(1)}, f32[4,2048]{1,0:T(4,128)S(1)}, f32[4,1536]{1,0:T(4,128)...) custom-call(bf16[2,16,32,768]{3,2,1,0:T(8,128)(2,1)S(1)} %get-tuple-, ...), custom_call_target="tpu_custom_call" | custom-call | tf_op jit(solution)/shard_map/reduce/pallas_call | solution.py:797
  121.1 54.1 %muon.1 = (f32[4,1536]{1,0:T(4,128)S(1)}, f32[4,512]{1,0:T(4,128)S(1)}, f32[4,2048]{1,0:T(4,128)S(1)}, f32[4,2048]{1,0:T(4,128)S(1)}) custom-call(f32[8,4,1024]{2,1,0:T(4,128)S(1)} %get-tuple-element.79.moments, f32[4,1536]{1,0:T(4,128)S(1)} %copy-done.9, f32[4,512]{1,0:T(4,128)S(1)} %copy-done.13, f32[4,2048]{1,0:T(4,128)S(1)} %copy-done.5, ...), custom_call_target="tpu_custom_call" | custom-call | tf_op jit(solution)/shard_map/muon/pallas_call | solution.py:975
  175.3 0.7 copy.52
  175.9 0.7 copy.53
  177.8 0.6 copy.56
  178.4 0.6 copy.57
  180.3 0.6 copy.60
  182.7 0.6 copy.64
  183.3 0.6 copy.65
  (54 shorter events, 5.3 us)
Async XLA Ops:
  4.9 56.5 %copy-start.16 = (s32[1,4]{1,0:T(1,128)S(1)}, s32[1,4]{1,0:T(1,128)}, u32[]{:S(2)}) copy-start(s32[1,4]{1,0:T(1,128)} %lengths.1) | copy-start | bytes 52
  4.9 0.9 copy-start
  5.8 0.9 copy-start.2
  6.7 0.8 copy-start.4
  7.4 0.8 copy-start.6
  8.2 0.7 copy-start.8
  8.9 0.7 copy-start.12
  75.8 20.1 %copy-start.1 = (bf16[128,512]{1,0:T(8,128)(2,1)S(1)}, bf16[128,512]{1,0:T(8,128)(2,1)}, u32[]{:S(2)}) copy-start(bf16[128,512]{1,0:T(8,128)(2,1)} %x_ref.3) | copy-start | bytes 393220
  75.8 20.1 %copy-start.3 = (bf16[128,512]{1,0:T(8,128)(2,1)S(1)}, bf16[128,512]{1,0:T(8,128)(2,1)}, u32[]{:S(2)}) copy-start(bf16[128,512]{1,0:T(8,128)(2,1)} %c_ref.3) | copy-start | bytes 393220
  75.8 20.1 %copy-start.10 = (f32[4,2048]{1,0:T(4,128)S(1)}, f32[4,2048]{1,0:T(4,128)}, u32[]{:S(2)}) copy-start(f32[4,2048]{1,0:T(4,128)} %m_expand.1) | copy-start | bytes 98308
  75.8 20.1 %copy-start.11 = (f32[4,2048]{1,0:T(4,128)S(1)}, f32[4,2048]{1,0:T(4,128)}, u32[]{:S(2)}) copy-start(f32[4,2048]{1,0:T(4,128)} %m_reduce.1) | copy-start | bytes 98308
  75.8 20.1 %copy-start.14 = (f32[4,1536]{1,0:T(4,128)S(1)}, f32[4,1536]{1,0:T(4,128)}, u32[]{:S(2)}) copy-start(f32[4,1536]{1,0:T(4,128)} %m_joint.1) | copy-start | bytes 73732
  75.8 20.1 %copy-start.15 = (f32[4,512]{1,0:T(4,128)S(1)}, f32[4,512]{1,0:T(4,128)}, u32[]{:S(2)}) copy-start(f32[4,512]{1,0:T(4,128)} %m_output.1) | copy-start | bytes 24580
  95.7 24.8 %copy-start.18 = (f32[11,4]{0,1:T(4,128)S(1)}, f32[11,4]{0,1:T(4,128)}, u32[]{:S(2)}) copy-start(f32[11,4]{0,1:T(4,128)} %param.25) | copy-start | bytes 532
  95.8 24.8 %copy-start.19 = (f32[11,4]{0,1:T(4,128)S(1)}, f32[11,4]{0,1:T(4,128)}, u32[]{:S(2)}) copy-start(f32[11,4]{0,1:T(4,128)} %param.26) | copy-start | bytes 532
  95.8 24.8 %copy-start.20 = (f32[11,4]{0,1:T(4,128)S(1)}, f32[11,4]{0,1:T(4,128)}, u32[]{:S(2)}) copy-start(f32[11,4]{0,1:T(4,128)} %param.27) | copy-start | bytes 532
  95.8 25.4 %copy-start.5 = (f32[4,2048]{1,0:T(4,128)S(1)}, f32[4,2048]{1,0:T(4,128)}, u32[]{:S(2)}) copy-start(f32[4,2048]{1,0:T(4,128)} %w_expand.1) | copy-start | bytes 98308
  95.8 25.3 %copy-start.7 = (f32[4,2048]{1,0:T(4,128)S(1)}, f32[4,2048]{1,0:T(4,128)}, u32[]{:S(2)}) copy-start(f32[4,2048]{1,0:T(4,128)} %w_reduce.1) | copy-start | bytes 98308
  95.8 25.3 %copy-start.9 = (f32[4,1536]{1,0:T(4,128)S(1)}, f32[4,1536]{1,0:T(4,128)}, u32[]{:S(2)}) copy-start(f32[4,1536]{1,0:T(4,128)} %w_joint.1) | copy-start | bytes 73732
  95.8 25.3 %copy-start.13 = (f32[4,512]{1,0:T(4,128)S(1)}, f32[4,512]{1,0:T(4,128)}, u32[]{:S(2)}) copy-start(f32[4,512]{1,0:T(4,128)} %w_output.1) | copy-start | bytes 24580
  120.5 63.4 %copy-start.17 = (f32[1,11,4]{1,2,0:T(4,128)}, f32[1,11,4]{1,2,0:T(4,128)S(1)}, u32[]{:S(2)}) copy-start(f32[1,11,4]{1,2,0:T(4,128)S(1)} %copy.36) | copy-start | bytes 532

commit v2 on v0

v2 whole, which is shorter than its diff:
```python
import math

import jax
import jax.numpy as jnp
from jax import lax
from jax.experimental import pallas as pl
from jax.experimental.pallas import tpu as pltpu
from jax.sharding import PartitionSpec as P

D = 512
HEADS = 8
FF = 2048
ROT = 16
HD = 64
STEP = 10

norm_epsilon = 1e-05
masked_score = -1e30
newton_first = 3.4445
newton_second = -4.775
newton_third = 2.0315
beta_first = 0.9
beta_second = 0.95
adam_epsilon = 1e-08
vector_rate = 0.2
muon_rate = 0.25
muon_beta = 0.95
muon_decay = 0.01
LOG2_E = 1.4426950408889634

BF = jnp.bfloat16
F32 = jnp.float32
MESH = pl.DeviceIdType.MESH
VMEM = pl.BlockSpec(memory_space=pltpu.VMEM)
SMEM = pl.BlockSpec(memory_space=pltpu.SMEM)
ANY = pl.BlockSpec(memory_space=pl.ANY)
WIDTHS = (3 * D, D, FF, FF)


def shape(dims, dtype):
    return jax.ShapeDtypeStruct(dims, dtype)


class Place:
    def __init__(self):
        self.z = lax.axis_index("fsdp")
        self.seq = lax.axis_index("seq")
        self.t = lax.axis_index("tensor")
        self.x = lax.div(self.seq, 2)
        self.c = lax.rem(self.seq, 2)
        self.d = 1 - 2 * self.c
        self.a = self.c * self.x + (1 - self.c) * self.z
        self.b = self.c * self.z + (1 - self.c) * self.x
        self.mate = self.x + 1 - 2 * lax.rem(self.x, 2)
        self.cross = 3 - self.x
        self.head = lax.div(self.x, 2)

    def at(self, z=None, x=None, c=None, t=None):
        z = self.z if z is None else z
        x = self.x if x is None else x
        c = self.c if c is None else c
        t = self.t if t is None else t
        return (z, 2 * x + c, t)

    def at_a(self, a):
        c = self.c
        return self.at(z=(1 - c) * a + c * self.z, x=c * a + (1 - c) * self.x)

    def at_b(self, b):
        c = self.c
        return self.at(z=c * b + (1 - c) * self.z, x=(1 - c) * b + c * self.x)

    def sibling(self):
        return self.at(c=1 - self.c)

    def octet(self):
        g = 4 * self.c + self.t
        members = [lax.rem(g + k, 8) for k in range(1, 8)]
        return [self.at(c=lax.div(m, 4), t=lax.rem(m, 4)) for m in members]

    def row_x(self):
        return [self.at(x=lax.rem(self.x + k, 4)) for k in range(1, 4)]

    def row_z(self):
        return [self.at(z=lax.rem(self.z + k, 4)) for k in range(1, 4)]

    def row_t(self):
        return [self.at(t=lax.rem(self.t + k, 4)) for k in range(1, 4)]


def ring(index, step):
    return lax.rem(index + step + 4, 4)


def greet(partners):
    barrier = pltpu.get_barrier_semaphore()
    for partner in partners:
        pl.semaphore_signal(barrier, inc=1, device_id=partner, device_id_type=MESH)
    return lambda: pl.semaphore_wait(barrier, len(partners))


class Wire:
    def __init__(self, send, recv, local):
        self.send = send
        self.recv = recv
        self.local = local
        self.count = 0
        self.loads = 0
        self.open = []

    def push(self, src, dst, device):
        index = self.count
        self.count += 1
        copy = pltpu.make_async_remote_copy(
            src_ref=src,
            dst_ref=dst,
            send_sem=self.send.at[index],
            recv_sem=self.recv.at[index],
            device_id=device,
            device_id_type=MESH,
        )
        copy.start()
        self.open.append(copy)
        return copy

    def load(self, src, dst):
        copy = pltpu.make_async_copy(src, dst, self.local.at[self.loads])
        self.loads += 1
        copy.start()
        return copy

    def drain(self):
        for copy in self.open:
            copy.wait_send()


def arrive(copies):
    for copy in copies:
        copy.wait_recv()


def dot(left, right):
    return jnp.dot(left, right, preferred_element_type=F32)


def dot_cols(left, right):
    return lax.dot_general(left, right, (((1,), (1,)), ((), ())), preferred_element_type=F32)


def dot_rows(left, right):
    return lax.dot_general(left, right, (((0,), (0,)), ((), ())), preferred_element_type=F32)


def turn(values, cosine, sine, sign):
    lane = lax.rem(lax.broadcasted_iota(jnp.int32, values.shape, 1), 64)
    crossed = jnp.where(lane < 8, -pltpu.roll(values, 120, 1), pltpu.roll(values, 8, 1))
    return values * cosine + crossed * (sine * sign)


def vec_row(v_ref, row):
    return jnp.concatenate([v_ref[k, row : row + 1, :] for k in range(4)], axis=1)


def normalise(rows):
    wide = rows.astype(F32)
    centred = wide - jnp.mean(wide, axis=-1, keepdims=True)
    variance = jnp.mean(centred * centred, axis=-1, keepdims=True)
    rate = lax.rsqrt(variance + norm_epsilon)
    return centred * rate, rate


def halves(values):
    high = values.astype(BF)
    return high, (values - high.astype(F32)).astype(BF)


def product(left_h, left_l, right_h, right_l):
    return dot(left_h, right_h) + (dot(left_h, right_l) + dot(left_l, right_h))


def spread_b(wire, place, ref):
    block = ref.at[place.c, place.a, place.b]
    return [wire.push(block, block, place.at_b(ring(place.b, k))) for k in range(1, 4)]


def spread_a(wire, place, ref):
    block = ref.at[place.c, place.a]
    return [wire.push(block, block, place.at_a(ring(place.a, k))) for k in range(1, 4)]


def ring_open(wire, place, ref):
    ups, downs = {}, {}
    for p, q in ((0, 2), (1, 3), (2, 0), (3, 1)):
        block = ref.at[place.c, place.a, p]
        ups[p] = wire.push(block, block, place.at_a(ring(place.a, 1)))
        block = ref.at[place.c, place.a, q]
        downs[q] = wire.push(block, block, place.at_a(ring(place.a, -1)))
    return ups, downs


def ring_pass(wire, place, ref, ups, downs):
    more = []
    for p, q in ((0, 2), (1, 3)):
        ups[p].wait_recv()
        block = ref.at[place.c, ring(place.a, -1), p]
        more.append(wire.push(block, block, place.at_a(ring(place.a, 1))))
        downs[q].wait_recv()
        block = ref.at[place.c, ring(place.a, 1), q]
        more.append(wire.push(block, block, place.at_a(ring(place.a, -1))))
    return more


def swap_part(wire, place, ref, step):
    block = ref.at[place.c, ring(place.a, step)]
    return wire.push(block, block, place.sibling())


def ring_close(wire, place, ref, ups, downs, more):
    arrive([ups[2], ups[3]])
    swaps = [swap_part(wire, place, ref, -1)]
    arrive([downs[0], downs[1]])
    swaps.append(swap_part(wire, place, ref, 1))
    arrive(more)
    swaps.append(swap_part(wire, place, ref, 2))
    return swaps


def swap_cores(wire, place, ref):
    return wire.push(ref.at[place.c], ref.at[place.c], place.sibling())


def natural(source, target, start, stop):
    for z in range(4):
        for x in range(4):
            target[8 * z + 2 * x] = source[0, z, x, :, start:stop]
            target[8 * z + 2 * x + 1] = source[1, x, z, :, start:stop]


def by_owner(target, z, rows, start, stop):
    for x in range(4):
        target[0, z, x, :, start:stop] = rows[32 * x : 32 * x + 16, :]
        target[1, x, z, :, start:stop] = rows[32 * x + 16 : 32 * x + 32, :]


def sum_cores(wire, place, ref, target):
    return wire.push(ref.at[1 - place.c], target, place.sibling())


def scatter_a(wire, place, ref, target):
    copies = []
    for k in range(1, 4):
        goal = ring(place.a, k)
        copies.append(wire.push(ref.at[goal], target.at[k - 1], place.at_a(goal)))
    return copies


def scatter_b(wire, place, ref, target):
    copies = []
    for k in range(1, 4):
        goal = ring(place.b, k)
        copies.append(wire.push(ref.at[goal], target.at[k - 1], place.at_b(goal)))
    return copies


def trade_t(wire, place, source, target):
    copies = []
    for k in range(1, 4):
        goal = ring(place.t, k)
        copies.append(wire.push(source.at[goal], target.at[place.t], place.at(t=goal)))
    return copies


def total(first, parts):
    value = first.astype(F32)
    for k in range(3):
        value = value + parts[k].astype(F32)
    return value


def unpair(target, part, k):
    one, two = part[:, 128:256], part[:, 256:384]
    target[:, 128 * k : 128 * k + 128] = part[:, 0:128]
    target[:, 512 + 128 * k : 640 + 128 * k] = jnp.concatenate(
        [one[:, 0:64], two[:, 0:64]], axis=1
    )
    target[:, 1024 + 128 * k : 1152 + 128 * k] = jnp.concatenate(
        [one[:, 64:128], two[:, 64:128]], axis=1
    )


INPUTS = (
    "lengths",
    "x",
    "c",
    "joint",
    "output",
    "expand",
    "reduce",
    "vectors",
    "m_joint",
    "m_output",
    "m_expand",
    "m_reduce",
    "first",
    "second",
)

OUTPUTS = (
    ("g_joint", (4, 1536), F32),
    ("g_output", (4, 512), F32),
    ("g_expand", (4, 2048), F32),
    ("g_reduce", (4, 2048), F32),
    ("n_joint", (4, 1536), F32),
    ("n_output", (4, 512), F32),
    ("n_expand", (4, 2048), F32),
    ("n_reduce", (4, 2048), F32),
    ("u_joint", (4, 1536), F32),
    ("u_output", (4, 512), F32),
    ("u_expand", (4, 2048), F32),
    ("u_reduce", (4, 2048), F32),
    ("block_output", (128, 512), BF),
    ("input_grad", (128, 512), F32),
    ("vector_grad", (4, 11), F32),
    ("second_next", (4, 11), F32),
    ("vector_next", (4, 11), F32),
)

SCRATCH = (
    ("joint_v", (4, 1536), F32),
    ("output_v", (4, 512), F32),
    ("expand_v", (4, 2048), F32),
    ("reduce_v", (4, 2048), F32),
    ("vectors_v", (4, 11), F32),
    ("first_v", (4, 11), F32),
    ("second_v", (4, 11), F32),
    ("table", (128, 128), F32),
    ("vec_sum", (4, 16, 128), F32),
    ("m_joint_v", (4, 1536), F32),
    ("m_output_v", (4, 512), F32),
    ("m_expand_v", (4, 2048), F32),
    ("m_reduce_v", (4, 2048), F32),
    ("w_out", (4, 4, 1920), F32),
    ("w_in", (4, 4, 1920), F32),
    ("w_rows", (16, 1920), F32),
    ("wj", (2, 4, 4, 16, 384), BF),
    ("wr", (2, 4, 4, 16, 1536), BF),
    ("w_joint", (32, 16, 384), BF),
    ("w_output", (32, 16, 512), BF),
    ("w_expand", (32, 16, 512), BF),
    ("w_reduce", (32, 16, 512), BF),
    ("v_own", (16, 128), F32),
    ("m_own", (4, 4, 2048), F32),
    ("m_early", (4, 4, 2048), F32),
    ("m_old", (16, 2048), F32),
    ("v_in", (8, 16, 128), F32),
    ("v_x", (4, 16, 128), F32),
    ("v", (4, 16, 128), F32),
    ("rows_x", (4, 128, 512), BF),
    ("rows_c", (4, 128, 512), BF),
    ("cos", (4, 128, 128), F32),
    ("sin", (4, 128, 128), F32),
    ("normed", (4, 128, 512), BF),
    ("query", (512, 128), F32),
    ("q_buf", (2, 512, 128), BF),
    ("kv_buf", (2, 512, 128), BF),
    ("qo", (2, 512, 128), BF),
    ("kv", (8, 512, 128), BF),
    ("hidden", (4, 128, 512), BF),
    ("pre", (4, 128, 512), BF),
    ("feed", (4, 128, 512), F32),
    ("row_grad", (4, 128, 512), F32),
    ("gf", (2, 4, 4, 16, 1024), BF),
    ("gf_core", (4, 4, 16, 1024), BF),
    ("gf_chip", (4, 4, 16, 1024), BF),
    ("gf_a", (3, 4, 16, 1024), BF),
    ("gf_line", (4, 16, 1024), BF),
    ("gf_b", (3, 16, 1024), BF),
    ("gf_out", (4, 4, 1024), F32),
    ("gf_in", (4, 4, 1024), F32),
    ("turned", (8, 128, 512), BF),
    ("scores", (9, 512, 512), F32),
    ("sums", (512, 128), F32),
    ("query_low", (2, 512, 128), BF),
    ("grad_low", (2, 512, 128), BF),
    ("out_turned", (2, 64, 512), F32),
    ("back_turned", (2, 64, 512), F32),
    ("centre", (2, 1, 512), F32),
    ("od", (2, 512, 128), BF),
    ("od_in", (2, 512, 128), BF),
    ("dk", (2, 4, 512, 128), BF),
    ("dk_in", (4, 512, 128), BF),
    ("dk_chip", (4, 512, 128), BF),
    ("dk_mate", (2, 512, 128), BF),
    ("dk_pass", (512, 128), BF),
    ("dk_cross", (512, 128), BF),
    ("dkv", (2, 512, 128), BF),
    ("pair_out", (512, 128), BF),
    ("joint_out", (512, 384), BF),
    ("out_cols", (4, 128, 128), BF),
    ("out_in", (4, 128, 128), BF),
    ("out_part", (4, 128, 512), BF),
    ("out_got", (4, 128, 512), BF),
    ("back_part", (4, 128, 512), BF),
    ("back_got", (4, 128, 512), BF),
    ("gj", (2, 4, 4, 16, 512), BF),
    ("gj_core", (4, 4, 16, 512), BF),
    ("gj_chip", (4, 4, 16, 512), BF),
    ("gj_a", (3, 4, 16, 512), BF),
    ("gj_line", (4, 16, 512), BF),
    ("gj_b", (3, 16, 512), BF),
    ("gj_out", (4, 4, 512), F32),
    ("gj_in", (4, 4, 512), F32),
    ("vp", (4, 4, 16, 128), F32),
    ("vp_core", (4, 16, 128), F32),
    ("vp_z", (3, 4, 16, 128), F32),
    ("vp_x", (3, 4, 16, 128), F32),
    ("vp_t", (3, 4, 16, 128), F32),
    ("gm_out", (4, 16, 512), F32),
    ("gm_in", (4, 16, 512), F32),
    ("m_rows", (16, 2048), F32),
    ("momentum", (2, 4, 4, 16, 2048), BF),
    ("gram", (512, 512), F32),
    ("gram_h", (512, 512), BF),
    ("gram_l", (512, 512), BF),
    ("poly_h", (512, 512), BF),
    ("poly_l", (512, 512), BF),
    ("temp_h", (512, 512), BF),
    ("temp_l", (512, 512), BF),
    ("u_out", (4, 4, 2048), F32),
    ("u_in", (4, 4, 2048), F32),
)

PUSHES = 192
LOADS = 16


class Box:
    pass


def attend_chunk(place, slot):
    return place.seq if slot == 0 else 7 - place.seq


def attend_score(slot, k):
    return 8 - k if slot == 0 else k


def attend_forward(r, place, slot):
    chunk = attend_chunk(place, slot)
    low = lax.broadcasted_iota(jnp.int32, (512, 128), 1) < 64
    packed = r.qo[slot].astype(F32)
    r.query_low[slot] = jnp.where(low, packed * (HD ** -0.5), 0.0).astype(BF)
    r.grad_low[slot] = jnp.where(low, 0.0, packed).astype(BF)
    out_grad = r.qo[slot].T[64:128, :].astype(F32)
    query = r.query_low[slot]
    index = 512 * chunk + lax.broadcasted_iota(jnp.int32, (1, 512), 1)
    begin = jnp.zeros((1, 512), jnp.int32)
    finish = 0
    for j in range(4):
        finish = finish + r.lengths[0, j]
        begin = jnp.where(index >= finish, finish, begin)

    def score(k, carry):
        top, total_sum = carry
        raw = dot_cols(r.kv[k], query) * LOG2_E
        key = lax.broadcasted_iota(jnp.int32, (512, 512), 0)
        allowed = (key <= index - 512 * k) & (key >= begin - 512 * k)
        raw = jnp.where(allowed, raw, masked_score)
        r.scores[attend_score(slot, k)] = raw
        higher = jnp.maximum(top, jnp.max(raw, axis=0, keepdims=True))
        part = jnp.sum(jnp.exp2(raw - higher), axis=0, keepdims=True)
        return higher, total_sum * jnp.exp2(top - higher) + part

    start = (jnp.full((1, 512), masked_score, F32), jnp.zeros((1, 512), F32))
    top, total_sum = lax.fori_loop(0, chunk + 1, score, start)
    level = top + jnp.log(total_sum) * LOG2_E

    def weigh(k, out):
        prob = jnp.exp2(r.scores[attend_score(slot, k)] - level)
        r.scores[attend_score(slot, k)] = prob
        return out + dot(r.turned[k, 64:128, :], prob.astype(BF))

    out = lax.fori_loop(0, chunk + 1, weigh, jnp.zeros((64, 512), F32))
    r.out_turned[slot] = out
    r.back_turned[slot] = jnp.zeros((64, 512), F32)
    r.centre[slot] = jnp.sum(out * out_grad, axis=0, keepdims=True)


def attend_backward(r, place, k):
    r.sums[...] = jnp.zeros_like(r.sums)
    for slot in range(2):

        @pl.when(k <= attend_chunk(place, slot))
        def _(slot=slot):
            prob = r.scores[attend_score(slot, k)]
            grad = dot_cols(r.kv[k], r.grad_low[slot])
            score_grad = (prob * (grad - r.centre[slot])).astype(BF)
            r.back_turned[slot] += dot(r.turned[k, 0:64, :], score_grad)
            r.sums[...] += dot(prob.astype(BF), r.grad_low[slot]) + dot(
                score_grad, r.query_low[slot]
            )

    return r.sums[...].astype(BF)


def attend_write(r, slot):
    both = jnp.concatenate([r.out_turned[slot], r.back_turned[slot] * (HD ** -0.5)], axis=0)
    r.od[slot] = both.T.astype(BF)


def newton(r, place):
    blocks, size = 1, 512

    def rows(i):
        return pl.ds(size * i, size)

    def diagonal(i):
        row = size * i + lax.broadcasted_iota(jnp.int32, (size, 512), 0)
        return row == lax.broadcasted_iota(jnp.int32, (size, 512), 1)

    def fill(i, trace):
        value = jnp.zeros((size, 512), F32)
        for k in range(4):
            lanes = slice(512 * k, 512 * k + 512)
            right = r.momentum[:, :, :, :, lanes].reshape(512, 512)
            value = value + dot_cols(right, right)
        r.gram[rows(i), :] = value
        return trace + jnp.sum(jnp.where(diagonal(i), value, 0.0), keepdims=True)

    trace = lax.fori_loop(0, blocks, fill, jnp.zeros((1, 1), F32))
    scale = 1.0 / (jnp.sqrt(trace) + 1e-07)

    def keep(value, i, high_ref, low_ref):
        high, small = halves(value)
        high_ref[rows(i), :] = high
        low_ref[rows(i), :] = small

    def prepare(i, _):
        value = r.gram[rows(i), :] * (scale * scale)
        r.gram[rows(i), :] = value
        keep(value, i, r.gram_h, r.gram_l)
        return 0

    lax.fori_loop(0, blocks, prepare, 0)

    def polynomial(i, _):
        square = product(r.gram_h[rows(i), :], r.gram_l[rows(i), :], r.gram_h[...], r.gram_l[...])
        value = (
            jnp.where(diagonal(i), newton_first, 0.0)
            + newton_second * r.gram[rows(i), :]
            + newton_third * square
        )
        keep(value, i, r.poly_h, r.poly_l)
        return 0

    def inner(i, _):
        value = product(r.gram_h[rows(i), :], r.gram_l[rows(i), :], r.poly_h[...], r.poly_l[...])
        keep(value, i, r.temp_h, r.temp_l)
        return 0

    def outer(i, _):
        value = product(r.temp_h[rows(i), :], r.temp_l[rows(i), :], r.poly_h[...], r.poly_l[...])
        r.gram[rows(i), :] = value
        keep(value, i, r.gram_h, r.gram_l)
        return 0

    def times(left, right_h, right_l):
        high, small = halves(left)
        return product(high, small, right_h[...], right_l[...])

    mine = pl.ds(pl.multiple_of(256 * place.c + 64 * place.a + 16 * place.b, 16), 16)
    own = None
    for sweep in range(4):
        lax.fori_loop(0, blocks, polynomial, 0)
        if sweep == 0:
            own = r.poly_h[mine, :].astype(F32) + r.poly_l[mine, :].astype(F32)
        else:
            own = times(own, r.poly_h, r.poly_l)
        if sweep < 3:
            lax.fori_loop(0, blocks, inner, 0)
            lax.fori_loop(0, blocks, outer, 0)

    def last_gram(left):
        left = times(left, r.gram_h, r.gram_l)
        left = times(left, r.poly_h, r.poly_l)
        return times(left, r.poly_h, r.poly_l)

    once = last_gram(own)
    own = newton_first * own + newton_second * once + newton_third * last_gram(once)
    return halves(own * scale)


def block_kernel(*refs):
    r = Box()
    names = list(INPUTS) + [n for n, _, _ in OUTPUTS] + [n for n, _, _ in SCRATCH]
    for name, ref in zip(names, refs):
        setattr(r, name, ref)
    place = Place()
    wire = Wire(*refs[-3:])
    z, x, c, t, d = place.z, place.x, place.c, place.t, place.d
    seq, mate, cross, head = place.seq, place.mate, place.cross, place.head
    sibling = place.sibling()

    met = greet(
        place.octet() + place.row_x() + place.row_z() + [place.at(x=cross, c=1 - c)]
    )

    load_w = [
        wire.load(r.joint, r.joint_v),
        wire.load(r.output, r.output_v),
        wire.load(r.expand, r.expand_v),
        wire.load(r.reduce, r.reduce_v),
    ]
    load_v = wire.load(r.vectors, r.vectors_v)
    load_x = wire.load(r.x, r.rows_x.at[t])
    load_c = wire.load(r.c, r.rows_c.at[t])
    load_m = [
        wire.load(r.m_joint, r.m_joint_v),
        wire.load(r.m_output, r.m_output_v),
        wire.load(r.m_expand, r.m_expand_v),
        wire.load(r.m_reduce, r.m_reduce_v),
        wire.load(r.first, r.first_v),
        wire.load(r.second, r.second_v),
    ]
    for copy in load_w:
        copy.wait()
    for k in range(4):
        for part in range(3):
            r.w_out[k, :, 128 * part : 128 * part + 128] = r.joint_v[
                :, 512 * part + 128 * k : 512 * part + 128 * k + 128
            ]
        r.w_out[k, :, 384:896] = r.output_v[...]
        r.w_out[k, :, 896:1408] = r.expand_v[:, 512 * k : 512 * k + 512]
        r.w_out[k, :, 1408:1920] = r.reduce_v[:, 512 * k : 512 * k + 512]
    load_v.wait()
    r.table[...] = jnp.zeros((128, 128), F32)
    column = lax.broadcasted_iota(jnp.int32, (128, 11), 0) - (16 * seq + 4 * t)
    own_vec = jnp.zeros((128, 11), F32)
    for j in range(4):
        own_vec = jnp.where(column == j, r.vectors_v[j : j + 1, :], own_vec)
    r.table[:, 0:11] = own_vec.astype(BF).astype(F32)
    r.v_own[...] = r.table[...].T[0:16, :]
    load_x.wait()
    load_c.wait()
    met()

    weights = trade_t(wire, place, r.w_out, r.w_in)
    octet = []
    for partner in place.octet():
        octet.append(wire.push(r.v_own, r.v_in.at[4 * c + t], partner))
    ahead, behind = ring(t, d), ring(t, -d)
    r.w_in[t] = r.w_out[t]
    r.v_in[4 * c + t] = r.v_own[...]
    arrive(weights)
    for k in range(4):
        r.w_rows[4 * k : 4 * k + 4, :] = r.w_in[k]
    keys, values = r.w_rows[:, 128:256], r.w_rows[:, 256:384]
    low16 = lax.broadcasted_iota(jnp.int32, (16, 128), 1) < 64
    r.wj[c, place.a, place.b, :, 0:128] = r.w_rows[:, 0:128].astype(BF)
    r.wj[c, place.a, place.b, :, 128:256] = jnp.where(
        low16, keys, pltpu.roll(values, 64, 1)
    ).astype(BF)
    r.wj[c, place.a, place.b, :, 256:384] = jnp.where(
        low16, pltpu.roll(keys, 64, 1), values
    ).astype(BF)
    joint_b = spread_b(wire, place, r.wj)
    x_first = wire.push(r.rows_x.at[t], r.rows_x.at[t], place.at(t=ahead))
    x_second = wire.push(r.rows_x.at[t], r.rows_x.at[t], place.at(t=behind))
    arrive(octet)
    vec = r.v_in[0]
    for k in range(1, 8):
        vec = vec + r.v_in[k]
    r.v_x[x] = vec
    vec_x = [wire.push(r.v_x.at[x], r.v_x.at[x], partner) for partner in place.row_x()]
    r.wr[c, place.a, place.b] = r.w_rows[:, 384:1920].astype(BF)
    rest_b = spread_b(wire, place, r.wr)

    half = ROT // 2
    lane = lax.rem(lax.broadcasted_iota(jnp.int32, (1, 128), 1), 64)
    frequency = jnp.zeros((1, 128), F32)
    for i in range(half):
        frequency = jnp.where(lax.rem(lane, half) == i, 10000.0 ** (-2.0 * i / ROT), frequency)
    frequency = jnp.where(lane < ROT, frequency, 0.0)

    def angles(i, _):
        index = 512 * seq + 128 * i + lax.broadcasted_iota(jnp.int32, (128, 1), 0)
        begin = jnp.zeros((128, 1), jnp.int32)
        finish = 0
        for j in range(4):
            finish = finish + r.lengths[0, j]
            begin = jnp.where(index >= finish, finish, begin)
        angle = (index - begin).astype(F32) * frequency
        r.cos[i] = jnp.cos(angle)
        r.sin[i] = jnp.sin(angle)
        return 0

    lax.fori_loop(0, 4, angles, 0)
    arrive(joint_b)
    joint_a = spread_a(wire, place, r.wj)
    arrive(vec_x)
    r.v[z] = (r.v_x[0] + r.v_x[1]) + (r.v_x[2] + r.v_x[3])
    vec_z = [wire.push(r.v.at[z], r.v.at[z], partner) for partner in place.row_z()]
    for copy in load_m:
        copy.wait()
    arrive(rest_b)
    rest_up, rest_down = ring_open(wire, place, r.wr)
    rest_swaps = [swap_part(wire, place, r.wr, 0)]
    x_first.wait_recv()
    x_third = wire.push(r.rows_x.at[behind], r.rows_x.at[behind], place.at(t=ahead))
    c_first = wire.push(r.rows_c.at[t], r.rows_c.at[t], place.at(t=ahead))
    c_second = wire.push(r.rows_c.at[t], r.rows_c.at[t], place.at(t=behind))
    arrive(joint_a)
    joint_swap = swap_cores(wire, place, r.wj)
    rest_more = ring_pass(wire, place, r.wr, rest_up, rest_down)
    arrive([joint_swap, *vec_z, x_second, x_third])
    natural(r.wj, r.w_joint, 0, 384)

    gain, shift = vec_row(r.v, 0), vec_row(r.v, 1)
    q_bias, k_bias, v_bias = r.v[t, 2:3, :], r.v[t, 3:4, :], r.v[t, 4:5, :]
    low_row = lax.broadcasted_iota(jnp.int32, (1, 128), 1) < 64
    pair_bias = (
        jnp.where(low_row, k_bias, pltpu.roll(v_bias, 64, 1)),
        jnp.where(low_row, pltpu.roll(k_bias, 64, 1), v_bias),
    )
    low = lax.broadcasted_iota(jnp.int32, (256, 128), 1) < 64

    def project(i, _):
        blocks, rows = pl.ds(2 * i, 2), pl.ds(256 * i, 256)
        normal, _rate = normalise(r.rows_x[blocks].reshape(256, 512))
        part = (normal * gain + shift).astype(BF)
        r.normed[blocks] = part.reshape(2, 128, 512)
        raw = dot(part, r.w_joint[...].reshape(512, 384))
        cosine, sine = r.cos[blocks].reshape(256, 128), r.sin[blocks].reshape(256, 128)
        r.query[rows, :] = turn(raw[:, 0:128] + q_bias, cosine, sine, 1.0)
        key_cos = jnp.where(low, cosine, 1.0)
        key_sin = jnp.where(low, sine, 0.0)
        for h in range(2):
            pair = raw[:, 128 + 128 * h : 256 + 128 * h] + pair_bias[h]
            r.kv_buf[h, rows, :] = turn(pair, key_cos, key_sin, 1.0).astype(BF)
        return 0

    lax.fori_loop(0, 2, project, 0)
    kv_cross = wire.push(r.kv_buf.at[1 - head], r.kv.at[seq], place.at(x=cross))
    kv_mate = wire.push(r.kv_buf.at[head], r.kv.at[seq], place.at(x=mate))
    kv_core = wire.push(r.kv_buf.at[head], r.kv.at[seq], sibling)
    r.kv[seq] = r.kv_buf[head]
    c_first.wait_recv()
    c_third = wire.push(r.rows_c.at[behind], r.rows_c.at[behind], place.at(t=ahead))
    rest_swaps += ring_close(wire, place, r.wr, rest_up, rest_down, rest_more)
    for k in range(4):
        lanes = slice(128 * k, 128 * k + 128)
        keys = r.m_joint_v[:, 512 + 128 * k : 640 + 128 * k]
        values = r.m_joint_v[:, 1024 + 128 * k : 1152 + 128 * k]
        r.m_own[0, :, 512 * k : 512 * k + 128] = r.m_joint_v[:, lanes]
        r.m_own[0, :, 512 * k + 128 : 512 * k + 256] = jnp.concatenate(
            [keys[:, 0:64], values[:, 0:64]], axis=1
        )
        r.m_own[0, :, 512 * k + 256 : 512 * k + 384] = jnp.concatenate(
            [keys[:, 64:128], values[:, 64:128]], axis=1
        )
        r.m_own[0, :, 512 * k + 384 : 512 * k + 512] = jnp.zeros((4, 128), F32)
        r.m_own[1, :, 512 * k : 512 * k + 128] = r.m_output_v[:, lanes]
        r.m_own[1, :, 512 * k + 128 : 512 * k + 512] = jnp.zeros((4, 384), F32)
    r.m_own[2] = r.m_expand_v[...]
    r.m_own[3] = r.m_reduce_v[...]
    arrive([c_second, c_third, *rest_swaps])
    natural(r.wr, r.w_output, 0, 512)
    natural(r.wr, r.w_expand, 512, 1024)
    natural(r.wr, r.w_reduce, 1024, 1536)
    out_rows = r.w_output[pl.ds(8 * t, 8)].reshape(128, 512)
    low = lax.broadcasted_iota(jnp.int32, (512, 128), 1) < 64
    grad = dot_cols(r.rows_c[...].reshape(512, 512), out_rows)
    query = r.query[...]
    r.q_buf[0] = jnp.where(low, query, pltpu.roll(grad, 64, 1)).astype(BF)
    r.q_buf[1] = jnp.where(low, pltpu.roll(query, 64, 1), grad).astype(BF)
    q_cross = wire.push(r.q_buf.at[1 - head], r.qo.at[1], place.at(x=cross, c=1 - c))
    early = trade_t(wire, place, r.m_own, r.m_early)
    r.qo[0] = r.q_buf[head]
    at_cross, at_mate = 2 * cross + c, 2 * mate + c
    at_far = 2 * (3 - mate) + c
    kv_cross.wait_recv()
    kv_far = wire.push(r.kv.at[at_cross], r.kv.at[at_cross], place.at(x=mate))
    kv_more = [kv_core, wire.push(r.kv.at[at_cross], r.kv.at[at_cross], sibling)]

    bias = jnp.concatenate([r.v[k, pl.ds(7 + t, 1), :] for k in range(4)], axis=1)

    def feed_forward(i, sums):
        blocks = pl.ds(2 * i, 2)
        part = r.normed[blocks].reshape(256, 512)
        wide = dot(part, r.w_expand[...].reshape(512, 512)) + bias
        square = wide * wide
        curve = jnp.tanh(0.7978845608 * (wide + 0.044715 * (square * wide)))
        r.hidden[blocks] = (0.5 * wide * (1.0 + curve)).astype(BF).reshape(2, 128, 512)
        slope = 0.5 * (1.0 + curve) + (0.5 * 0.7978845608) * wide * (1.0 - curve * curve) * (
            1.0 + (3 * 0.044715) * square
        )
        part = r.rows_c[blocks].reshape(256, 512)
        back = dot(part, r.w_reduce[...].reshape(512, 512))
        grad = (back * slope).astype(BF)
        r.pre[blocks] = grad.reshape(2, 128, 512)
        return sums + jnp.sum(grad.astype(F32), axis=0, keepdims=True)

    hidden_sum = lax.fori_loop(0, 2, feed_forward, jnp.zeros((1, 512), F32))
    kv_mate.wait_recv()
    kv_more.append(wire.push(r.kv.at[at_mate], r.kv.at[at_mate], sibling))
    for j in range(4):
        lanes = slice(128 * j, 128 * j + 128)
        expand_grad = dot_rows(
            r.normed[:, :, lanes].reshape(512, 128), r.pre[...].reshape(512, 512)
        )
        by_owner(r.gf, j, expand_grad.astype(BF), 0, 512)
        reduce_grad = dot_rows(
            r.rows_c[:, :, lanes].reshape(512, 128), r.hidden[...].reshape(512, 512)
        )
        by_owner(r.gf, j, reduce_grad.astype(BF), 512, 1024)
    gf_swap = sum_cores(wire, place, r.gf, r.gf_core)
    kv_far.wait_recv()
    kv_more.append(wire.push(r.kv.at[at_far], r.kv.at[at_far], sibling))

    arrive(early)
    r.m_early[t] = r.m_own[t]
    for k in range(4):
        r.m_old[4 * k : 4 * k + 4, :] = r.m_early[k]
    gf_swap.wait_recv()
    for a in range(4):
        r.gf_chip[a] = (r.gf[c, a].astype(F32) + r.gf_core[a].astype(F32)).astype(BF)
    gf_a = scatter_a(wire, place, r.gf_chip, r.gf_a)
    arrive(kv_more)

    for k in range(8):
        r.turned[k] = r.kv[k].T
    attend_forward(r, place, 0)
    q_cross.wait_recv()
    arrive(gf_a)
    r.gf_line[...] = total(r.gf_chip[place.a], r.gf_a).astype(BF)
    gf_b = scatter_b(wire, place, r.gf_line, r.gf_b)
    attend_forward(r, place, 1)

    far = 3 - mate
    dk_swap = []

    def chip_sum(index):
        return r.dk[c, index].astype(F32) + r.dk_in[index].astype(F32)

    for step, column in enumerate((far, mate, cross, x)):

        def key_block(p, _, column=column):
            parity = lax.rem(1 - c + p, 2)
            r.dk[parity, column] = attend_backward(r, place, 2 * column + parity)
            return 0

        lax.fori_loop(0, 2, key_block, 0)
        dk_swap.append(wire.push(r.dk.at[1 - c, column], r.dk_in.at[column], sibling))
        if step == 1:
            dk_swap[0].wait_recv()
            r.dk_chip[0] = chip_sum(far).astype(BF)
            dk_far = wire.push(r.dk_chip.at[0], r.dk_mate.at[0], place.at(x=mate))
        if step == 2:
            dk_swap[1].wait_recv()
            r.dk_chip[1] = chip_sum(mate).astype(BF)
            dk_near = wire.push(r.dk_chip.at[1], r.dk_mate.at[1], place.at(x=mate))
    attend_write(r, 1)
    od_cross = wire.push(r.od.at[1], r.od_in.at[head], place.at(x=cross, c=1 - c))
    attend_write(r, 0)
    r.od_in[head] = r.od[0]

    arrive(gf_b)
    gf_own = total(r.gf_line[place.b], r.gf_b)
    for k in range(4):
        r.gf_out[k] = gf_own[4 * k : 4 * k + 4, :]
    r.gm_out[2] = gf_own[:, 0:512]
    r.gm_out[3] = gf_own[:, 512:1024]
    gf_t = trade_t(wire, place, r.gf_out, r.gf_in)
    r.gf_in[t] = r.gf_out[t]
    low = lax.broadcasted_iota(jnp.int32, (128, 128), 1) < 64
    dk_swap[2].wait_recv()
    dk_far.wait_recv()
    r.dk_pass[...] = (chip_sum(cross) + r.dk_mate[0].astype(F32)).astype(BF)
    dk_cross = wire.push(r.dk_pass, r.dk_cross, place.at(x=cross))

    def feed_out(i, _):
        blocks = pl.ds(2 * i, 2)
        part = r.hidden[blocks].reshape(256, 512)
        r.feed[blocks] = dot_cols(part, r.w_reduce[...].reshape(512, 512)).reshape(2, 128, 512)
        part = r.pre[blocks].reshape(256, 512)
        r.row_grad[blocks] = dot_cols(part, r.w_expand[...].reshape(512, 512)).reshape(2, 128, 512)
        return 0

    lax.fori_loop(0, 2, feed_out, 0)
    od_cross.wait_recv()
    for i in range(4):
        rows = pl.ds(128 * i, 128)
        left = r.od_in[0, rows, :].astype(F32)
        right = r.od_in[1, rows, :].astype(F32)
        joined = jnp.where(low, left, pltpu.roll(right, 64, 1)).astype(BF)
        r.pair_out[rows, :] = joined
        back = jnp.where(low, pltpu.roll(left, 64, 1), right)
        r.joint_out[rows, 0:128] = turn(back, r.cos[i], r.sin[i], -1.0).astype(BF)
    for i in range(4):
        rows = pl.ds(128 * i, 128)
        out_rows = r.w_output[pl.ds(8 * t, 8)].reshape(128, 512)
        r.out_part[i] = (r.feed[i] + dot(r.pair_out[rows, :], out_rows)).astype(BF)
    for j in range(4):
        part = r.rows_c[:, :, 128 * j : 128 * j + 128].reshape(512, 128)
        r.out_cols[j] = dot_rows(r.pair_out[...], part).astype(BF)
    out_cols = trade_t(wire, place, r.out_cols, r.out_in)
    out_parts = trade_t(wire, place, r.out_part, r.out_got)
    r.out_in[t] = r.out_cols[t]
    r.out_got[t] = r.out_part[t]
    arrive([dk_swap[3], dk_near])
    r.dkv[head] = (chip_sum(x) + r.dk_mate[1].astype(F32)).astype(BF)
    dk_cross.wait_recv()
    r.dkv[1 - head] = r.dk_cross[...]
    for h in range(2):
        for i in range(4):
            rows = pl.ds(128 * i, 128)
            key_cos = jnp.where(low, r.cos[i], 1.0)
            key_sin = jnp.where(low, r.sin[i], 0.0)
            r.joint_out[rows, 128 + 128 * h : 256 + 128 * h] = turn(
                r.dkv[h, rows, :].astype(F32), key_cos, key_sin, -1.0
            ).astype(BF)
    arrive(out_cols)
    for j in range(4):
        part = r.normed[:, :, 128 * j : 128 * j + 128].reshape(512, 128)
        by_owner(r.gj, j, dot_rows(part, r.joint_out[...]).astype(BF), 0, 384)
        by_owner(r.gj, j, r.out_in[j], 384, 512)
    gj_swap = sum_cores(wire, place, r.gj, r.gj_core)

    r.vp[0] = jnp.zeros((4, 16, 128), F32)
    shift_sum = jnp.zeros((1, 512), F32)
    gain_sum = jnp.zeros((1, 512), F32)
    for i in range(4):
        rows = pl.ds(128 * i, 128)
        part = r.row_grad[i] + dot_cols(r.joint_out[rows, :], r.w_joint[...].reshape(512, 384))
        r.back_part[i] = part.astype(BF)
        normal, _rate = normalise(r.rows_x[i])
        shift_sum = shift_sum + jnp.sum(part, axis=0, keepdims=True)
        gain_sum = gain_sum + jnp.sum(part * normal, axis=0, keepdims=True)
    gj_swap.wait_recv()
    for a in range(4):
        r.gj_chip[a] = (r.gj[c, a].astype(F32) + r.gj_core[a].astype(F32)).astype(BF)
    gj_a = scatter_a(wire, place, r.gj_chip, r.gj_a)
    back_parts = trade_t(wire, place, r.back_part, r.back_got)
    r.back_got[t] = r.back_part[t]
    out_sum = jnp.sum(r.rows_c[t].astype(F32), axis=0, keepdims=True)
    joint_sum = jnp.sum(r.joint_out[...].astype(F32), axis=0, keepdims=True)
    one, two = joint_sum[:, 128:256], joint_sum[:, 256:384]
    for k in range(4):
        lanes = slice(128 * k, 128 * k + 128)
        r.vp[0, k, 0:1, :] = gain_sum[:, lanes]
        r.vp[0, k, 1:2, :] = shift_sum[:, lanes]
        r.vp[0, k, 5:6, :] = out_sum[:, lanes]
        r.vp[0, k, 6:7, :] = out_sum[:, lanes]
        r.vp[0, k, pl.ds(7 + t, 1), :] = hidden_sum[:, lanes]
    r.vp[0, t, 2:3, :] = joint_sum[:, 0:128]
    r.vp[0, t, 3:4, :] = jnp.where(low_row, one, pltpu.roll(two, 64, 1))
    r.vp[0, t, 4:5, :] = jnp.where(low_row, pltpu.roll(one, 64, 1), two)
    vp_swap = wire.push(r.vp.at[0], r.vp_core, sibling)
    arrive(gj_a)
    r.gj_line[...] = total(r.gj_chip[place.a], r.gj_a).astype(BF)
    gj_b = scatter_b(wire, place, r.gj_line, r.gj_b)
    vp_swap.wait_recv()
    r.vp[1] = r.vp[0] + r.vp_core[...]
    vp_z = [wire.push(r.vp.at[1], r.vp_z.at[k], p) for k, p in enumerate(place.row_z())]

    arrive(gj_b)
    gj_own = total(r.gj_line[place.b], r.gj_b)
    r.gm_out[0, :, 0:384] = gj_own[:, 0:384]
    r.gm_out[0, :, 384:512] = jnp.zeros((16, 128), F32)
    r.gm_out[1, :, 0:128] = gj_own[:, 384:512]
    r.gm_out[1, :, 128:512] = jnp.zeros((16, 384), F32)
    gm_t = trade_t(wire, place, r.gm_out, r.gm_in)
    r.gm_in[t] = r.gm_out[t]
    for k in range(4):
        r.gj_out[k] = gj_own[4 * k : 4 * k + 4, :]
    gj_t = trade_t(wire, place, r.gj_out, r.gj_in)
    r.gj_in[t] = r.gj_out[t]
    arrive(vp_z)
    r.vp[2] = total(r.vp[1], r.vp_z)
    vp_x = [wire.push(r.vp.at[2], r.vp_x.at[k], p) for k, p in enumerate(place.row_x())]

    arrive(gm_t)
    for k in range(4):
        lanes = slice(512 * k, 512 * k + 512)
        value = muon_beta * r.m_old[:, lanes] + r.gm_in[k]
        r.momentum[c, place.a, place.b, :, lanes] = value.astype(BF)
    m_b = spread_b(wire, place, r.momentum)

    arrive(gf_t)
    for k in range(4):
        part = r.gf_in[k]
        r.g_expand[:, 512 * k : 512 * k + 512] = part[:, 0:512]
        r.g_reduce[:, 512 * k : 512 * k + 512] = part[:, 512:1024]
    arrive(gj_t)
    for k in range(4):
        lanes = slice(128 * k, 128 * k + 128)
        part = r.gj_in[k]
        unpair(r.g_joint, part, k)
        r.g_output[:, lanes] = part[:, 384:512]
    for old, grad, new in (
        (r.m_joint_v, r.g_joint, r.n_joint),
        (r.m_output_v, r.g_output, r.n_output),
        (r.m_expand_v, r.g_expand, r.n_expand),
        (r.m_reduce_v, r.g_reduce, r.n_reduce),
    ):
        new[...] = muon_beta * old[...] + grad[...]
    arrive(vp_x)
    r.vp[3] = total(r.vp[2], r.vp_x)
    vp_t = [wire.push(r.vp.at[3], r.vp_t.at[k], p) for k, p in enumerate(place.row_t())]
    arrive(out_parts)
    arrive(back_parts)
    arrive(m_b)
    m_up, m_down = ring_open(wire, place, r.momentum)
    m_swaps = [swap_part(wire, place, r.momentum, 0)]
    m_more = ring_pass(wire, place, r.momentum, m_up, m_down)
    wide = r.rows_x[t].astype(F32)
    feed = r.out_got[0].astype(F32)
    back = r.back_got[0].astype(F32)
    for k in range(1, 4):
        feed = feed + r.out_got[k].astype(F32)
        back = back + r.back_got[k].astype(F32)
    r.block_output[...] = (wide + feed + vec_row(r.v, 5) + vec_row(r.v, 6)).astype(BF)
    normal, rate = normalise(r.rows_x[t])
    scaled = back * gain
    mean_one = jnp.mean(scaled, axis=-1, keepdims=True)
    mean_two = jnp.mean(scaled * normal, axis=-1, keepdims=True)
    r.input_grad[...] = r.rows_c[t].astype(F32) + rate * (scaled - mean_one - normal * mean_two)
    m_swaps += ring_close(wire, place, r.momentum, m_up, m_down, m_more)
    arrive(vp_t)
    r.vec_sum[...] = total(r.vp[3], r.vp_t)
    r.table[0:16, :] = r.vec_sum[z]
    r.table[...] = r.table[...].T
    vector_grad = r.table[pl.ds(pl.multiple_of(16 * seq + 4 * t, 4), 4), 0:11]
    r.vector_grad[...] = vector_grad
    first_next = beta_first * r.first_v[...] + (1.0 - beta_first) * vector_grad
    second_next = (
        beta_second * r.second_v[...] + (1.0 - beta_second) * vector_grad * vector_grad
    )
    r.second_next[...] = second_next
    first_hat = first_next / (1.0 - beta_first**STEP)
    second_hat = second_next / (1.0 - beta_second**STEP)
    r.vector_next[...] = r.vectors_v[...] - vector_rate * first_hat / (
        jnp.sqrt(second_hat) + adam_epsilon
    )
    arrive(m_swaps)

    high, small = newton(r, place)
    for k in range(4):
        lanes = slice(512 * k, 512 * k + 512)
        columns = r.momentum[:, :, :, :, lanes].reshape(512, 512)
        r.m_rows[:, lanes] = dot(high, columns) + dot(small, columns)
    for k in range(4):
        r.u_out[k] = r.m_rows[4 * k : 4 * k + 4, :]
    u_t = trade_t(wire, place, r.u_out, r.u_in)
    r.u_in[t] = r.u_out[t]
    arrive(u_t)
    for k in range(4):
        lanes = slice(128 * k, 128 * k + 128)
        unpair(r.u_joint, r.u_in[0, :, 512 * k : 512 * k + 384], k)
        r.u_output[:, lanes] = r.u_in[1, :, 512 * k : 512 * k + 128]
    for k, (old, change, new) in enumerate(
        (
            (r.joint_v, r.u_joint, r.u_joint),
            (r.output_v, r.u_output, r.u_output),
            (r.expand_v, r.u_in.at[2], r.u_expand),
            (r.reduce_v, r.u_in.at[3], r.u_reduce),
        )
    ):
        factor = muon_rate * 0.2 * math.sqrt(max(D, WIDTHS[k]))
        new[...] = old[...] * (1.0 - muon_rate * muon_decay) - factor * change[...]
    wire.drain()


def block_stage(*arrays):
    return pl.pallas_call(
        block_kernel,
        out_shape=tuple(shape(dims, dtype) for _, dims, dtype in OUTPUTS),
        in_specs=[SMEM] + [ANY] * (len(INPUTS) - 1),
        out_specs=(VMEM,) * len(OUTPUTS),
        scratch_shapes=[pltpu.VMEM(dims, dtype) for _, dims, dtype in SCRATCH]
        + [
            pltpu.SemaphoreType.DMA((PUSHES,)),
            pltpu.SemaphoreType.DMA((PUSHES,)),
            pltpu.SemaphoreType.DMA((LOADS,)),
        ],
        compiler_params=pltpu.CompilerParams(
            collective_id=1, has_side_effects=True, vmem_limit_bytes=56 << 20
        ),
        name="block",
    )(*arrays)


def write_kernel(*refs):
    count = len(OUTPUTS)
    sem = refs[-1]
    copies = []
    for k in range(count):
        copy = pltpu.make_async_copy(refs[k], refs[count + k], sem.at[k])
        copy.start()
        copies.append(copy)
    for copy in copies:
        copy.wait()


def write_stage(*arrays):
    count = len(arrays)
    return pl.pallas_call(
        write_kernel,
        out_shape=tuple(shape(a.shape, a.dtype) for a in arrays),
        in_specs=[VMEM] * count,
        out_specs=(ANY,) * count,
        scratch_shapes=[pltpu.SemaphoreType.DMA((count,))],
        name="write",
    )(*arrays)


def shards(
    block_input,
    cotangent,
    doc_lengths,
    joint_weight,
    output_weight,
    expand_weight,
    reduce_weight,
    joint_moment,
    output_moment,
    expand_moment,
    reduce_moment,
    vectors,
    first_moment,
    second_moment,
):
    results = block_stage(
        doc_lengths, block_input, cotangent, joint_weight, output_weight, expand_weight,
        reduce_weight, vectors.T, joint_moment, output_moment, expand_moment, reduce_moment,
        first_moment.T, second_moment.T,
    )
    results = write_stage(*results)
    return (*results[12:14], *results[0:12], *[part.T for part in results[14:]])


def solution(mesh):
    rows = P(("fsdp", "seq", "tensor"), None)
    columns = P(None, ("fsdp", "seq", "tensor"))
    return jax.shard_map(
        shards,
        mesh=mesh,
        in_specs=(rows, rows, P("fsdp", None)) + (rows,) * 8 + (columns,) * 3,
        out_specs=(rows,) * 14 + (columns,) * 3,
        check_vma=False,
    )
```

time: 838 us -> 119 us (0.14)
  waiting for transfers between devices: 267 us -> 0 us
  blocking collectives: 224 us -> 0 us
  matrix products: 149 us -> 0 us
  Pallas kernels: 0 us -> 118 us
  other arithmetic: 64.3 us -> 0 us
  local copies, waits for them, and re-layouts: 57.8 us -> 0 us
  starting transfers between devices: 50.4 us -> 0 us
  between operations: 16.9 us -> 0.83 us
    unnamed x10 -> x0, waiting for transfers between devices: 220 us -> none
    all_gather x6 -> x0, blocking collectives: 149 us -> none  [the longest x1 55.2 us: shards(): lax.all_gather(output_weight.astype(jnp.bfloat16), ('fsdp', 'seq', 'tenso...]
    dot_general x42 -> x0, matrix products: 149 us -> none  [the longest x5 38.1 us: orthogonalize(): gram_matrix = jnp.dot(current, current.T, precision=highest)]
    pallas_call x0 -> x2, Pallas kernels: none -> 118 us  [the longest x1 116 us: block_stage(): pl.pallas_call(block_kernel, out_shape=tuple((shape(dims, dtype) for _, d...]
    unnamed x1 -> x0, blocking collectives: 66.5 us -> none
    all_to_all x9 -> x0, starting transfers between devices: 50.1 us -> none  [the longest x1 10.4 us: shards(): lax.all_to_all(query_grads.reshape(query_count, heads_here, HD).astype(jn...]
    reduce_scatter x2 -> x0, waiting for transfers between devices: 25.7 us -> none  [the longest x1 21.4 us: shards(): lax.psum_scatter(combined.astype(jnp.bfloat16), 'tensor', scatter_dimensi...]
    convert_element_type x10 -> x0, other arithmetic: 24.2 us -> none  [the longest x2 19.8 us: backward_block(): score_grad = (probability * (prob_grad - centre)).astype(jnp.bfloat16)]
  transfers between devices with their start and end apart: 17 -> 0, of which waited for: 10 -> 0; matrix products, arithmetic and copies ran while one was open for 19% -> 0% of each run, Pallas kernels for 0% -> 0%
where the time goes in v2:
time: 119 us
  Pallas kernels  118 us (99%)
    pallas_call x1, Pallas kernels, block_stage(): pl.pallas_call(block_kernel, out_shape=tuple((shape(dims, dtype) for _, d...  116 us

profile of v2, /device:TPU:1, one launch (start us, length us, event | category | flops | bytes accessed | tf_op | source)
XLA Modules:
  0.0 119.1 jit_solution(8003811139557995225)
XLA Ops:
  0.7 116.0 %block.1 = (f32[4,1536]{1,0:T(4,128)}, f32[4,512]{1,0:T(4,128)}, f32[4,2048]{1,0:T(4,128)}, f32[4,2048]{1,0:T(4,128)}, f32[4,1536]{1,0:T(4,128)}, /*index=5*/f32...) custom-call(s32[1,4]{1,0:T(1,128)} %refs_0_.1, ...), custom_call_target="tpu_custom_call" | custom-call | tf_op jit(solution)/shard_map/block/pallas_call | solution.py:1076
  116.7 2.2 %write.1 = (f32[4,1536]{1,0:T(4,128)}, f32[4,512]{1,0:T(4,128)}, f32[4,2048]{1,0:T(4,128)}, f32[4,2048]{1,0:T(4,128)}, f32[4,1536]{1,0:T(4,128)}, /*index=5*/f32...) custom-call(f32[4,1536]{1,0:T(4,128)} %get-tuple-element.51.refs_0_,, ...), custom_call_target="tpu_custom_call" | custom-call | tf_op jit(solution)/shard_map/write/pallas_call | solution.py:1108

commit v3 on v2

--- a/solution.py
+++ b/solution.py
@@ -69,6 +69,15 @@
     def at_b(self, b):
         c = self.c
         return self.at(z=c * b + (1 - c) * self.z, x=(1 - c) * b + c * self.x)
+
+    def at_ab(self, a, b):
+        c = self.c
+        return self.at(z=(1 - c) * a + c * b, x=c * a + (1 - c) * b)
+
+    def plane(self):
+        steps = [(i, j) for i in range(4) for j in range(4) if i + j > 0]
+        steps.sort(key=lambda step: -min(step[0], 4 - step[0]) - min(step[1], 4 - step[1]))
+        return [(ring(self.a, i), ring(self.b, j)) for i, j in steps]
 
     def sibling(self):
         return self.at(c=1 - self.c)
@@ -123,6 +132,21 @@
         self.open.append(copy)
         return copy
 
+    def offer(self, first, source, target, sender, goal, device):
+        return pltpu.make_async_remote_copy(
+            src_ref=source,
+            dst_ref=target,
+            send_sem=self.send.at[first + goal],
+            recv_sem=self.recv.at[first + sender],
+            device_id=device,
+            device_id_type=MESH,
+        )
+
+    def block(self, count):
+        first = self.count
+        self.count += count
+        return first
+
     def load(self, src, dst):
         copy = pltpu.make_async_copy(src, dst, self.local.at[self.loads])
         self.loads += 1
@@ -178,14 +202,14 @@
     return dot(left_h, right_h) + (dot(left_h, right_l) + dot(left_l, right_h))
 
 
+def squared(high, small):
+    cross = dot(high, small)
+    return dot(high, high) + (cross + cross.T)
+
+
 def spread_b(wire, place, ref):
     block = ref.at[place.c, place.a, place.b]
     return [wire.push(block, block, place.at_b(ring(place.b, k))) for k in range(1, 4)]
-
-
-def spread_a(wire, place, ref):
-    block = ref.at[place.c, place.a]
-    return [wire.push(block, block, place.at_a(ring(place.a, k))) for k in range(1, 4)]
 
 
 def ring_open(wire, place, ref):
@@ -225,6 +249,25 @@
     return swaps
 
 
+def spread_plane(wire, place, ref):
+    block = ref.at[place.c, place.a, place.b]
+    return [wire.push(block, block, place.at_ab(a, b)) for a, b in place.plane()]
+
+
+def scatter_plane(wire, place, ref, target):
+    copies = []
+    for k, (a, b) in enumerate(place.plane()):
+        copies.append(wire.push(ref.at[a, b], target.at[k], place.at_ab(a, b)))
+    return copies
+
+
+def add_plane(first, parts):
+    value = first.astype(F32)
+    for k in range(15):
+        value = value + parts[k].astype(F32)
+    return value
+
+
 def swap_cores(wire, place, ref):
     return wire.push(ref.at[place.c], ref.at[place.c], place.sibling())
 
@@ -244,22 +287,6 @@
 
 def sum_cores(wire, place, ref, target):
     return wire.push(ref.at[1 - place.c], target, place.sibling())
-
-
-def scatter_a(wire, place, ref, target):
-    copies = []
-    for k in range(1, 4):
-        goal = ring(place.a, k)
-        copies.append(wire.push(ref.at[goal], target.at[k - 1], place.at_a(goal)))
-    return copies
-
-
-def scatter_b(wire, place, ref, target):
-    copies = []
-    for k in range(1, 4):
-        goal = ring(place.b, k)
-        copies.append(wire.push(ref.at[goal], target.at[k - 1], place.at_b(goal)))
-    return copies
 
 
 def trade_t(wire, place, source, target):
@@ -339,10 +366,13 @@
     ("m_output_v", (4, 512), F32),
     ("m_expand_v", (4, 2048), F32),
     ("m_reduce_v", (4, 2048), F32),
-    ("w_out", (4, 4, 1920), F32),
-    ("w_in", (4, 4, 1920), F32),
-    ("w_rows", (16, 1920), F32),
-    ("wj", (2, 4, 4, 16, 384), BF),
+    ("j_out", (4, 4, 384), F32),
+    ("j_in", (4, 4, 384), F32),
+    ("j_rows", (16, 384), F32),
+    ("w_out", (4, 4, 1536), F32),
+    ("w_in", (4, 4, 1536), F32),
+    ("w_rows", (16, 1536), F32),
+    ("wj", (2, 4, 4, 16, 512), BF),
     ("wr", (2, 4, 4, 16, 1536), BF),
     ("w_joint", (32, 16, 384), BF),
     ("w_output", (32, 16, 512), BF),
@@ -352,8 +382,7 @@
     ("m_own", (4, 4, 2048), F32),
     ("m_early", (4, 4, 2048), F32),
     ("m_old", (16, 2048), F32),
-    ("v_in", (8, 16, 128), F32),
-    ("v_x", (4, 16, 128), F32),
+    ("v_in", (4, 16, 128), F32),
     ("v", (4, 16, 128), F32),
     ("rows_x", (4, 128, 512), BF),
     ("rows_c", (4, 128, 512), BF),
@@ -372,21 +401,25 @@
     ("gf", (2, 4, 4, 16, 1024), BF),
     ("gf_core", (4, 4, 16, 1024), BF),
     ("gf_chip", (4, 4, 16, 1024), BF),
-    ("gf_a", (3, 4, 16, 1024), BF),
-    ("gf_line", (4, 16, 1024), BF),
-    ("gf_b", (3, 16, 1024), BF),
-    ("gf_out", (4, 4, 1024), F32),
-    ("gf_in", (4, 4, 1024), F32),
+    ("gf_in", (15, 16, 1024), BF),
+    ("go", (2, 4, 4, 16, 128), BF),
+    ("go_core", (4, 4, 16, 128), BF),
+    ("go_chip", (4, 4, 16, 128), BF),
+    ("go_in", (15, 16, 128), BF),
+    ("early_out", (4, 4, 1152), F32),
+    ("early_in", (4, 4, 1152), F32),
     ("turned", (8, 128, 512), BF),
+    ("keys", (8, 512, 128), BF),
     ("scores", (9, 512, 512), F32),
-    ("sums", (512, 128), F32),
+    ("sums", (2, 512, 128), F32),
     ("query_low", (2, 512, 128), BF),
     ("grad_low", (2, 512, 128), BF),
-    ("out_turned", (2, 64, 512), F32),
     ("back_turned", (2, 64, 512), F32),
     ("centre", (2, 1, 512), F32),
-    ("od", (2, 512, 128), BF),
-    ("od_in", (2, 512, 128), BF),
+    ("out_low", (2, 64, 512), BF),
+    ("out_heads", (2, 64, 512), BF),
+    ("back_low", (2, 64, 512), BF),
+    ("back_heads", (2, 64, 512), BF),
     ("dk", (2, 4, 512, 128), BF),
     ("dk_in", (4, 512, 128), BF),
     ("dk_chip", (4, 512, 128), BF),
@@ -394,7 +427,7 @@
     ("dk_pass", (512, 128), BF),
     ("dk_cross", (512, 128), BF),
     ("dkv", (2, 512, 128), BF),
-    ("pair_out", (512, 128), BF),
+    ("pair_out", (128, 512), BF),
     ("joint_out", (512, 384), BF),
     ("out_cols", (4, 128, 128), BF),
     ("out_in", (4, 128, 128), BF),
@@ -402,23 +435,22 @@
     ("out_got", (4, 128, 512), BF),
     ("back_part", (4, 128, 512), BF),
     ("back_got", (4, 128, 512), BF),
-    ("gj", (2, 4, 4, 16, 512), BF),
-    ("gj_core", (4, 4, 16, 512), BF),
-    ("gj_chip", (4, 4, 16, 512), BF),
-    ("gj_a", (3, 4, 16, 512), BF),
-    ("gj_line", (4, 16, 512), BF),
-    ("gj_b", (3, 16, 512), BF),
-    ("gj_out", (4, 4, 512), F32),
-    ("gj_in", (4, 4, 512), F32),
+    ("gj", (2, 4, 4, 16, 384), BF),
+    ("gj_core", (4, 4, 16, 384), BF),
+    ("gj_chip", (4, 4, 16, 384), BF),
+    ("gj_in", (15, 16, 384), BF),
+    ("late_out", (4, 4, 384), F32),
+    ("late_in", (4, 4, 384), F32),
     ("vp", (4, 4, 16, 128), F32),
     ("vp_core", (4, 16, 128), F32),
     ("vp_z", (3, 4, 16, 128), F32),
     ("vp_x", (3, 4, 16, 128), F32),
     ("vp_t", (3, 4, 16, 128), F32),
-    ("gm_out", (4, 16, 512), F32),
-    ("gm_in", (4, 16, 512), F32),
+    ("gm_out", (4, 16, 512), BF),
+    ("gm_in", (4, 16, 512), BF),
     ("m_rows", (16, 2048), F32),
-    ("momentum", (2, 4, 4, 16, 2048), BF),
+    ("momentum", (2, 4, 4, 16, 1536), BF),
+    ("extra", (2, 4, 4, 16, 512), BF),
     ("gram", (512, 512), F32),
     ("gram_h", (512, 512), BF),
     ("gram_l", (512, 512), BF),
@@ -426,11 +458,13 @@
     ("poly_l", (512, 512), BF),
     ("temp_h", (512, 512), BF),
     ("temp_l", (512, 512), BF),
-    ("u_out", (4, 4, 2048), F32),
-    ("u_in", (4, 4, 2048), F32),
+    ("u_rows", (4, 16, 512), F32),
+    ("u_out", (4, 16, 512), BF),
+    ("u_in", (4, 16, 512), BF),
+    ("u_wide", (4, 4, 2048), F32),
 )
 
-PUSHES = 192
+PUSHES = 240
 LOADS = 16
 
 
@@ -444,6 +478,17 @@
 
 def attend_score(slot, k):
     return 8 - k if slot == 0 else k
+
+
+def pairs(count, step, carry):
+    def two(k, carry):
+        return step(2 * k + 1, step(2 * k, carry))
+
+    def one(_, carry):
+        return step(count - 1, carry)
+
+    carry = lax.fori_loop(0, lax.div(count, 2), two, carry)
+    return lax.fori_loop(0, lax.rem(count, 2), one, carry)
 
 
 def attend_forward(r, place, slot):
@@ -453,7 +498,9 @@
     r.query_low[slot] = jnp.where(low, packed * (HD ** -0.5), 0.0).astype(BF)
     r.grad_low[slot] = jnp.where(low, 0.0, packed).astype(BF)
     out_grad = r.qo[slot].T[64:128, :].astype(F32)
-    query = r.query_low[slot]
+    high, small = halves(packed * (HD ** -0.5 * LOG2_E))
+    high, small = high.astype(F32), small.astype(F32)
+    query = jnp.where(low, high, pltpu.roll(small, 64, 1)).astype(BF)
     index = 512 * chunk + lax.broadcasted_iota(jnp.int32, (1, 512), 1)
     begin = jnp.zeros((1, 512), jnp.int32)
     finish = 0
@@ -461,11 +508,13 @@
         finish = finish + r.lengths[0, j]
         begin = jnp.where(index >= finish, finish, begin)
 
-    def score(k, carry):
+    def score(k, carry, last=False):
         top, total_sum = carry
-        raw = dot_cols(r.kv[k], query) * LOG2_E
+        raw = dot_cols(r.keys[k], query)
         key = lax.broadcasted_iota(jnp.int32, (512, 512), 0)
-        allowed = (key <= index - 512 * k) & (key >= begin - 512 * k)
+        allowed = key >= begin - 512 * k
+        if last:
+            allowed = allowed & (key <= lax.broadcasted_iota(jnp.int32, (512, 512), 1))
         raw = jnp.where(allowed, raw, masked_score)
         r.scores[attend_score(slot, k)] = raw
         higher = jnp.maximum(top, jnp.max(raw, axis=0, keepdims=True))
@@ -473,7 +522,7 @@
         return higher, total_sum * jnp.exp2(top - higher) + part
 
     start = (jnp.full((1, 512), masked_score, F32), jnp.zeros((1, 512), F32))
-    top, total_sum = lax.fori_loop(0, chunk + 1, score, start)
+    top, total_sum = score(chunk, pairs(chunk, score, start), last=True)
     level = top + jnp.log(total_sum) * LOG2_E
 
     def weigh(k, out):
@@ -481,32 +530,40 @@
         r.scores[attend_score(slot, k)] = prob
         return out + dot(r.turned[k, 64:128, :], prob.astype(BF))
 
-    out = lax.fori_loop(0, chunk + 1, weigh, jnp.zeros((64, 512), F32))
-    r.out_turned[slot] = out
+    out = pairs(chunk + 1, weigh, jnp.zeros((64, 512), F32))
+    r.out_low[slot] = out.astype(BF)
     r.back_turned[slot] = jnp.zeros((64, 512), F32)
     r.centre[slot] = jnp.sum(out * out_grad, axis=0, keepdims=True)
 
 
-def attend_backward(r, place, k):
+def attend_backward(r, place, column):
     r.sums[...] = jnp.zeros_like(r.sums)
-    for slot in range(2):
-
-        @pl.when(k <= attend_chunk(place, slot))
-        def _(slot=slot):
-            prob = r.scores[attend_score(slot, k)]
-            grad = dot_cols(r.kv[k], r.grad_low[slot])
-            score_grad = (prob * (grad - r.centre[slot])).astype(BF)
-            r.back_turned[slot] += dot(r.turned[k, 0:64, :], score_grad)
-            r.sums[...] += dot(prob.astype(BF), r.grad_low[slot]) + dot(
-                score_grad, r.query_low[slot]
-            )
-
-    return r.sums[...].astype(BF)
-
-
-def attend_write(r, slot):
-    both = jnp.concatenate([r.out_turned[slot], r.back_turned[slot] * (HD ** -0.5)], axis=0)
-    r.od[slot] = both.T.astype(BF)
+
+    def both_slots(slot, _):
+        chunk = (1 - slot) * place.seq + slot * (7 - place.seq)
+        out_grad, query, centre = r.grad_low[slot], r.query_low[slot], r.centre[slot]
+
+        def block(part):
+            k = 2 * column + part
+            prob = r.scores[(1 - slot) * (8 - k) + slot * k]
+            grad = dot_cols(r.kv[k], out_grad)
+            score_grad = (prob * (grad - centre)).astype(BF)
+            r.sums[part] += dot(prob.astype(BF), out_grad) + dot(score_grad, query)
+            return dot(r.turned[k, 0:64, :], score_grad)
+
+        @pl.when(2 * column + 1 <= chunk)
+        def _():
+            r.back_turned[slot] += block(0) + block(1)
+
+        @pl.when(2 * column == chunk)
+        def _():
+            r.back_turned[slot] += block(0)
+
+        return 0
+
+    lax.fori_loop(0, 2, both_slots, 0)
+    r.dk[0, column] = r.sums[0].astype(BF)
+    r.dk[1, column] = r.sums[1].astype(BF)
 
 
 def newton(r, place):
@@ -521,11 +578,18 @@
 
     def fill(i, trace):
         value = jnp.zeros((size, 512), F32)
-        for k in range(4):
+        for k in range(3):
             lanes = slice(512 * k, 512 * k + 512)
             right = r.momentum[:, :, :, :, lanes].reshape(512, 512)
             value = value + dot_cols(right, right)
         r.gram[rows(i), :] = value
+
+        @pl.when(place.t >= 2)
+        def _():
+            right = r.extra[...].reshape(512, 512)
+            r.gram[rows(i), :] += dot_cols(right, right)
+
+        value = r.gram[rows(i), :]
         return trace + jnp.sum(jnp.where(diagonal(i), value, 0.0), keepdims=True)
 
     trace = lax.fori_loop(0, blocks, fill, jnp.zeros((1, 1), F32))
@@ -545,7 +609,7 @@
     lax.fori_loop(0, blocks, prepare, 0)
 
     def polynomial(i, _):
-        square = product(r.gram_h[rows(i), :], r.gram_l[rows(i), :], r.gram_h[...], r.gram_l[...])
+        square = squared(r.gram_h[...], r.gram_l[...])
         value = (
             jnp.where(diagonal(i), newton_first, 0.0)
             + newton_second * r.gram[rows(i), :]
@@ -555,12 +619,12 @@
         return 0
 
     def inner(i, _):
-        value = product(r.gram_h[rows(i), :], r.gram_l[rows(i), :], r.poly_h[...], r.poly_l[...])
+        value = squared(r.poly_h[...], r.poly_l[...])
         keep(value, i, r.temp_h, r.temp_l)
         return 0
 
     def outer(i, _):
-        value = product(r.temp_h[rows(i), :], r.temp_l[rows(i), :], r.poly_h[...], r.poly_l[...])
+        value = product(r.gram_h[...], r.gram_l[...], r.temp_h[...], r.temp_l[...])
         r.gram[rows(i), :] = value
         keep(value, i, r.gram_h, r.gram_l)
         return 0
@@ -603,7 +667,9 @@
     sibling = place.sibling()
 
     met = greet(
-        place.octet() + place.row_x() + place.row_z() + [place.at(x=cross, c=1 - c)]
+        place.octet()
+        + [place.at_ab(a, b) for a, b in place.plane()]
+        + [place.at(x=cross, c=1 - c)]
     )
 
     load_w = [
@@ -627,12 +693,12 @@
         copy.wait()
     for k in range(4):
         for part in range(3):
-            r.w_out[k, :, 128 * part : 128 * part + 128] = r.joint_v[
+            r.j_out[k, :, 128 * part : 128 * part + 128] = r.joint_v[
                 :, 512 * part + 128 * k : 512 * part + 128 * k + 128
             ]
-        r.w_out[k, :, 384:896] = r.output_v[...]
-        r.w_out[k, :, 896:1408] = r.expand_v[:, 512 * k : 512 * k + 512]
-        r.w_out[k, :, 1408:1920] = r.reduce_v[:, 512 * k : 512 * k + 512]
+        r.w_out[k, :, 0:512] = r.output_v[...]
+        r.w_out[k, :, 512:1024] = r.expand_v[:, 512 * k : 512 * k + 512]
+        r.w_out[k, :, 1024:1536] = r.reduce_v[:, 512 * k : 512 * k + 512]
     load_v.wait()
     r.table[...] = jnp.zeros((128, 128), F32)
     column = lax.broadcasted_iota(jnp.int32, (128, 11), 0) - (16 * seq + 4 * t)
@@ -645,35 +711,29 @@
     load_c.wait()
     met()
 
-    weights = trade_t(wire, place, r.w_out, r.w_in)
-    octet = []
-    for partner in place.octet():
-        octet.append(wire.push(r.v_own, r.v_in.at[4 * c + t], partner))
-    ahead, behind = ring(t, d), ring(t, -d)
+    joint_t = trade_t(wire, place, r.j_out, r.j_in)
+    for partner in place.row_t():
+        joint_t.append(wire.push(r.v_own, r.v_in.at[t], partner))
+    rest_t = trade_t(wire, place, r.w_out, r.w_in)
+    r.j_in[t] = r.j_out[t]
+    r.v_in[t] = r.v_own[...]
     r.w_in[t] = r.w_out[t]
-    r.v_in[4 * c + t] = r.v_own[...]
-    arrive(weights)
+    arrive(joint_t)
+    for k in range(4):
+        r.j_rows[4 * k : 4 * k + 4, :] = r.j_in[k]
+    keys, values = r.j_rows[:, 128:256], r.j_rows[:, 256:384]
+    low16 = lax.broadcasted_iota(jnp.int32, (16, 128), 1) < 64
+    own_block = r.wj.at[c, place.a, place.b]
+    own_block[:, 0:128] = r.j_rows[:, 0:128].astype(BF)
+    own_block[:, 128:256] = jnp.where(low16, keys, pltpu.roll(values, 64, 1)).astype(BF)
+    own_block[:, 256:384] = jnp.where(low16, pltpu.roll(keys, 64, 1), values).astype(BF)
+    own_block[:, 384:512] = ((r.v_in[0] + r.v_in[1]) + (r.v_in[2] + r.v_in[3])).astype(BF)
+    joint_all = spread_plane(wire, place, r.wj)
+    x_rows = [wire.push(r.rows_x.at[t], r.rows_x.at[t], p) for p in place.row_t()]
+    arrive(rest_t)
     for k in range(4):
         r.w_rows[4 * k : 4 * k + 4, :] = r.w_in[k]
-    keys, values = r.w_rows[:, 128:256], r.w_rows[:, 256:384]
-    low16 = lax.broadcasted_iota(jnp.int32, (16, 128), 1) < 64
-    r.wj[c, place.a, place.b, :, 0:128] = r.w_rows[:, 0:128].astype(BF)
-    r.wj[c, place.a, place.b, :, 128:256] = jnp.where(
-        low16, keys, pltpu.roll(values, 64, 1)
-    ).astype(BF)
-    r.wj[c, place.a, place.b, :, 256:384] = jnp.where(
-        low16, pltpu.roll(keys, 64, 1), values
-    ).astype(BF)
-    joint_b = spread_b(wire, place, r.wj)
-    x_first = wire.push(r.rows_x.at[t], r.rows_x.at[t], place.at(t=ahead))
-    x_second = wire.push(r.rows_x.at[t], r.rows_x.at[t], place.at(t=behind))
-    arrive(octet)
-    vec = r.v_in[0]
-    for k in range(1, 8):
-        vec = vec + r.v_in[k]
-    r.v_x[x] = vec
-    vec_x = [wire.push(r.v_x.at[x], r.v_x.at[x], partner) for partner in place.row_x()]
-    r.wr[c, place.a, place.b] = r.w_rows[:, 384:1920].astype(BF)
+    r.wr[c, place.a, place.b] = r.w_rows[...].astype(BF)
     rest_b = spread_b(wire, place, r.wr)
 
     half = ROT // 2
@@ -696,24 +756,21 @@
         return 0
 
     lax.fori_loop(0, 4, angles, 0)
-    arrive(joint_b)
-    joint_a = spread_a(wire, place, r.wj)
-    arrive(vec_x)
-    r.v[z] = (r.v_x[0] + r.v_x[1]) + (r.v_x[2] + r.v_x[3])
-    vec_z = [wire.push(r.v.at[z], r.v.at[z], partner) for partner in place.row_z()]
     for copy in load_m:
         copy.wait()
+    c_rows = [wire.push(r.rows_c.at[t], r.rows_c.at[t], p) for p in place.row_t()]
+    arrive(joint_all)
+    joint_swap = swap_cores(wire, place, r.wj)
     arrive(rest_b)
     rest_up, rest_down = ring_open(wire, place, r.wr)
     rest_swaps = [swap_part(wire, place, r.wr, 0)]
-    x_first.wait_recv()
-    x_third = wire.push(r.rows_x.at[behind], r.rows_x.at[behind], place.at(t=ahead))
-    c_first = wire.push(r.rows_c.at[t], r.rows_c.at[t], place.at(t=ahead))
-    c_second = wire.push(r.rows_c.at[t], r.rows_c.at[t], place.at(t=behind))
-    arrive(joint_a)
-    joint_swap = swap_cores(wire, place, r.wj)
-    rest_more = ring_pass(wire, place, r.wr, rest_up, rest_down)
-    arrive([joint_swap, *vec_z, x_second, x_third])
+    arrive([joint_swap, *x_rows])
+    for k in range(4):
+        own_vec = jnp.zeros((16, 128), F32)
+        for i in range(4):
+            for part in (r.wj[0, k, i, :, 384:512], r.wj[1, i, k, :, 384:512]):
+                own_vec = own_vec + part.astype(F32)
+        r.v[k] = own_vec
     natural(r.wj, r.w_joint, 0, 384)
 
     gain, shift = vec_row(r.v, 0), vec_row(r.v, 1)
@@ -745,26 +802,31 @@
     kv_mate = wire.push(r.kv_buf.at[head], r.kv.at[seq], place.at(x=mate))
     kv_core = wire.push(r.kv_buf.at[head], r.kv.at[seq], sibling)
     r.kv[seq] = r.kv_buf[head]
-    c_first.wait_recv()
-    c_third = wire.push(r.rows_c.at[behind], r.rows_c.at[behind], place.at(t=ahead))
+    rest_more = ring_pass(wire, place, r.wr, rest_up, rest_down)
     rest_swaps += ring_close(wire, place, r.wr, rest_up, rest_down, rest_more)
     for k in range(4):
         lanes = slice(128 * k, 128 * k + 128)
         keys = r.m_joint_v[:, 512 + 128 * k : 640 + 128 * k]
         values = r.m_joint_v[:, 1024 + 128 * k : 1152 + 128 * k]
-        r.m_own[0, :, 512 * k : 512 * k + 128] = r.m_joint_v[:, lanes]
-        r.m_own[0, :, 512 * k + 128 : 512 * k + 256] = jnp.concatenate(
+        start = 384 * k
+        r.m_own[0, :, start : start + 128] = r.m_joint_v[:, lanes]
+        r.m_own[0, :, start + 128 : start + 256] = jnp.concatenate(
             [keys[:, 0:64], values[:, 0:64]], axis=1
         )
-        r.m_own[0, :, 512 * k + 256 : 512 * k + 384] = jnp.concatenate(
+        r.m_own[0, :, start + 256 : start + 384] = jnp.concatenate(
             [keys[:, 64:128], values[:, 64:128]], axis=1
         )
-        r.m_own[0, :, 512 * k + 384 : 512 * k + 512] = jnp.zeros((4, 128), F32)
-        r.m_own[1, :, 512 * k : 512 * k + 128] = r.m_output_v[:, lanes]
-        r.m_own[1, :, 512 * k + 128 : 512 * k + 512] = jnp.zeros((4, 384), F32)
+    r.m_own[0, :, 1536:2048] = jnp.zeros((4, 512), F32)
+    r.m_own[1, :, 0:512] = r.m_output_v[...]
+    r.m_own[1, :, 512:2048] = jnp.zeros((4, 1536), F32)
     r.m_own[2] = r.m_expand_v[...]
     r.m_own[3] = r.m_reduce_v[...]
-    arrive([c_second, c_third, *rest_swaps])
+    at_cross, at_mate = 2 * cross + c, 2 * mate + c
+    at_far = 2 * (3 - mate) + c
+    kv_cross.wait_recv()
+    kv_far = wire.push(r.kv.at[at_cross], r.kv.at[at_cross], place.at(x=mate))
+    kv_more = [kv_core, wire.push(r.kv.at[at_cross], r.kv.at[at_cross], sibling)]
+    arrive([*c_rows, *rest_swaps])
     natural(r.wr, r.w_output, 0, 512)
     natural(r.wr, r.w_expand, 512, 1024)
     natural(r.wr, r.w_reduce, 1024, 1536)
@@ -777,11 +839,6 @@
     q_cross = wire.push(r.q_buf.at[1 - head], r.qo.at[1], place.at(x=cross, c=1 - c))
     early = trade_t(wire, place, r.m_own, r.m_early)
     r.qo[0] = r.q_buf[head]
-    at_cross, at_mate = 2 * cross + c, 2 * mate + c
-    at_far = 2 * (3 - mate) + c
-    kv_cross.wait_recv()
-    kv_far = wire.push(r.kv.at[at_cross], r.kv.at[at_cross], place.at(x=mate))
-    kv_more = [kv_core, wire.push(r.kv.at[at_cross], r.kv.at[at_cross], sibling)]
 
     bias = jnp.concatenate([r.v[k, pl.ds(7 + t, 1), :] for k in range(4)], axis=1)
 
@@ -825,17 +882,18 @@
     gf_swap.wait_recv()
     for a in range(4):
         r.gf_chip[a] = (r.gf[c, a].astype(F32) + r.gf_core[a].astype(F32)).astype(BF)
-    gf_a = scatter_a(wire, place, r.gf_chip, r.gf_a)
-    arrive(kv_more)
-
+    arrive([*kv_more, q_cross])
+    gf_all = scatter_plane(wire, place, r.gf_chip, r.gf_in)
+
+    low = lax.broadcasted_iota(jnp.int32, (512, 128), 1) < 64
     for k in range(8):
         r.turned[k] = r.kv[k].T
+        wide = r.kv[k].astype(F32)
+        r.keys[k] = jnp.where(low, wide, pltpu.roll(wide, 64, 1)).astype(BF)
+    attend_forward(r, place, 1)
+    out_cross = wire.push(r.out_low.at[1], r.out_heads.at[head], place.at(x=cross, c=1 - c))
     attend_forward(r, place, 0)
-    q_cross.wait_recv()
-    arrive(gf_a)
-    r.gf_line[...] = total(r.gf_chip[place.a], r.gf_a).astype(BF)
-    gf_b = scatter_b(wire, place, r.gf_line, r.gf_b)
-    attend_forward(r, place, 1)
+    r.out_heads[head] = r.out_low[0]
 
     far = 3 - mate
     dk_swap = []
@@ -844,14 +902,17 @@
         return r.dk[c, index].astype(F32) + r.dk_in[index].astype(F32)
 
     for step, column in enumerate((far, mate, cross, x)):
-
-        def key_block(p, _, column=column):
-            parity = lax.rem(1 - c + p, 2)
-            r.dk[parity, column] = attend_backward(r, place, 2 * column + parity)
-            return 0
-
-        lax.fori_loop(0, 2, key_block, 0)
+        attend_backward(r, place, column)
         dk_swap.append(wire.push(r.dk.at[1 - c, column], r.dk_in.at[column], sibling))
+        if step == 0:
+            out_cross.wait_recv()
+            turned = r.out_heads[...].reshape(128, 512)
+            r.pair_out[...] = turned
+            out_grad = dot(turned, r.rows_c[...].reshape(512, 512)).astype(BF)
+            for j in range(4):
+                r.out_cols[j] = out_grad[:, 128 * j : 128 * j + 128]
+            out_cols = trade_t(wire, place, r.out_cols, r.out_in)
+            r.out_in[t] = r.out_cols[t]
         if step == 1:
             dk_swap[0].wait_recv()
             r.dk_chip[0] = chip_sum(far).astype(BF)
@@ -860,25 +921,22 @@
             dk_swap[1].wait_recv()
             r.dk_chip[1] = chip_sum(mate).astype(BF)
             dk_near = wire.push(r.dk_chip.at[1], r.dk_mate.at[1], place.at(x=mate))
-    attend_write(r, 1)
-    od_cross = wire.push(r.od.at[1], r.od_in.at[head], place.at(x=cross, c=1 - c))
-    attend_write(r, 0)
-    r.od_in[head] = r.od[0]
-
-    arrive(gf_b)
-    gf_own = total(r.gf_line[place.b], r.gf_b)
-    for k in range(4):
-        r.gf_out[k] = gf_own[4 * k : 4 * k + 4, :]
-    r.gm_out[2] = gf_own[:, 0:512]
-    r.gm_out[3] = gf_own[:, 512:1024]
-    gf_t = trade_t(wire, place, r.gf_out, r.gf_in)
-    r.gf_in[t] = r.gf_out[t]
-    low = lax.broadcasted_iota(jnp.int32, (128, 128), 1) < 64
-    dk_swap[2].wait_recv()
-    dk_far.wait_recv()
+            arrive(out_cols)
+            for j in range(4):
+                by_owner(r.go, j, r.out_in[j], 0, 128)
+            go_swap = sum_cores(wire, place, r.go, r.go_core)
+    for slot in range(2):
+        r.back_low[slot] = (r.back_turned[slot] * (HD ** -0.5)).astype(BF)
+    back_cross = wire.push(r.back_low.at[1], r.back_heads.at[head], place.at(x=cross, c=1 - c))
+    r.back_heads[head] = r.back_low[0]
+    go_swap.wait_recv()
+    for a in range(4):
+        r.go_chip[a] = (r.go[c, a].astype(F32) + r.go_core[a].astype(F32)).astype(BF)
+    go_all = scatter_plane(wire, place, r.go_chip, r.go_in)
+
+    arrive([dk_swap[2], dk_far])
     r.dk_pass[...] = (chip_sum(cross) + r.dk_mate[0].astype(F32)).astype(BF)
     dk_cross = wire.push(r.dk_pass, r.dk_cross, place.at(x=cross))
-
     def feed_out(i, _):
         blocks = pl.ds(2 * i, 2)
         part = r.hidden[blocks].reshape(256, 512)
@@ -888,26 +946,18 @@
         return 0
 
     lax.fori_loop(0, 2, feed_out, 0)
-    od_cross.wait_recv()
-    for i in range(4):
-        rows = pl.ds(128 * i, 128)
-        left = r.od_in[0, rows, :].astype(F32)
-        right = r.od_in[1, rows, :].astype(F32)
-        joined = jnp.where(low, left, pltpu.roll(right, 64, 1)).astype(BF)
-        r.pair_out[rows, :] = joined
-        back = jnp.where(low, pltpu.roll(left, 64, 1), right)
-        r.joint_out[rows, 0:128] = turn(back, r.cos[i], r.sin[i], -1.0).astype(BF)
-    for i in range(4):
-        rows = pl.ds(128 * i, 128)
-        out_rows = r.w_output[pl.ds(8 * t, 8)].reshape(128, 512)
-        r.out_part[i] = (r.feed[i] + dot(r.pair_out[rows, :], out_rows)).astype(BF)
-    for j in range(4):
-        part = r.rows_c[:, :, 128 * j : 128 * j + 128].reshape(512, 128)
-        r.out_cols[j] = dot_rows(r.pair_out[...], part).astype(BF)
-    out_cols = trade_t(wire, place, r.out_cols, r.out_in)
+    out_rows = r.w_output[pl.ds(8 * t, 8)].reshape(128, 512)
+    for i in range(2):
+        blocks, lanes = slice(2 * i, 2 * i + 2), slice(256 * i, 256 * i + 256)
+        part = r.feed[blocks].reshape(256, 512) + dot_rows(r.pair_out[:, lanes], out_rows)
+        r.out_part[blocks] = part.astype(BF).reshape(2, 128, 512)
     out_parts = trade_t(wire, place, r.out_part, r.out_got)
-    r.out_in[t] = r.out_cols[t]
     r.out_got[t] = r.out_part[t]
+    back_cross.wait_recv()
+    back = r.back_heads[...].reshape(128, 512).astype(F32).T
+    cosine, sine = r.cos[...].reshape(512, 128), r.sin[...].reshape(512, 128)
+    r.joint_out[:, 0:128] = turn(back, cosine, sine, -1.0).astype(BF)
+    low = lax.broadcasted_iota(jnp.int32, (128, 128), 1) < 64
     arrive([dk_swap[3], dk_near])
     r.dkv[head] = (chip_sum(x) + r.dk_mate[1].astype(F32)).astype(BF)
     dk_cross.wait_recv()
@@ -920,11 +970,9 @@
             r.joint_out[rows, 128 + 128 * h : 256 + 128 * h] = turn(
                 r.dkv[h, rows, :].astype(F32), key_cos, key_sin, -1.0
             ).astype(BF)
-    arrive(out_cols)
     for j in range(4):
         part = r.normed[:, :, 128 * j : 128 * j + 128].reshape(512, 128)
         by_owner(r.gj, j, dot_rows(part, r.joint_out[...]).astype(BF), 0, 384)
-        by_owner(r.gj, j, r.out_in[j], 384, 512)
     gj_swap = sum_cores(wire, place, r.gj, r.gj_core)
 
     r.vp[0] = jnp.zeros((4, 16, 128), F32)
@@ -940,7 +988,7 @@
     gj_swap.wait_recv()
     for a in range(4):
         r.gj_chip[a] = (r.gj[c, a].astype(F32) + r.gj_core[a].astype(F32)).astype(BF)
-    gj_a = scatter_a(wire, place, r.gj_chip, r.gj_a)
+    gj_all = scatter_plane(wire, place, r.gj_chip, r.gj_in)
     back_parts = trade_t(wire, place, r.back_part, r.back_got)
     r.back_got[t] = r.back_part[t]
     out_sum = jnp.sum(r.rows_c[t].astype(F32), axis=0, keepdims=True)
@@ -957,47 +1005,105 @@
     r.vp[0, t, 3:4, :] = jnp.where(low_row, one, pltpu.roll(two, 64, 1))
     r.vp[0, t, 4:5, :] = jnp.where(low_row, pltpu.roll(one, 64, 1), two)
     vp_swap = wire.push(r.vp.at[0], r.vp_core, sibling)
-    arrive(gj_a)
-    r.gj_line[...] = total(r.gj_chip[place.a], r.gj_a).astype(BF)
-    gj_b = scatter_b(wire, place, r.gj_line, r.gj_b)
+    arrive(gf_all)
+    gf_own = add_plane(r.gf_chip[place.a, place.b], r.gf_in)
+    arrive(go_all)
+    go_own = add_plane(r.go_chip[place.a, place.b], r.go_in)
+    for k in range(4):
+        r.early_out[k, :, 0:1024] = gf_own[4 * k : 4 * k + 4, :]
+        r.early_out[k, :, 1024:1152] = go_own[4 * k : 4 * k + 4, :]
+    r.gm_out[1, :, 0:128] = go_own.astype(BF)
+    r.gm_out[2] = gf_own[:, 0:512].astype(BF)
+    r.gm_out[3] = gf_own[:, 512:1024].astype(BF)
+    gm_first = wire.block(4)
+    gm_widths = (384, 128, 512, 512)
+
+    def to_newton(w, sender):
+        lanes = slice(0, gm_widths[w])
+        return wire.offer(
+            gm_first, r.gm_out.at[w, :, lanes], r.gm_in.at[sender, :, lanes], sender, w,
+            place.at(t=w),
+        )
+
+    def send_newton(w):
+        @pl.when(t != w)
+        def _():
+            to_newton(w, t).start()
+
+        @pl.when(t == w)
+        def _():
+            r.gm_in[w, :, 0 : gm_widths[w]] = r.gm_out[w, :, 0 : gm_widths[w]]
+
+    for w in (1, 2, 3):
+        send_newton(w)
+    early_t = trade_t(wire, place, r.early_out, r.early_in)
+    r.early_in[t] = r.early_out[t]
+
     vp_swap.wait_recv()
     r.vp[1] = r.vp[0] + r.vp_core[...]
     vp_z = [wire.push(r.vp.at[1], r.vp_z.at[k], p) for k, p in enumerate(place.row_z())]
 
-    arrive(gj_b)
-    gj_own = total(r.gj_line[place.b], r.gj_b)
-    r.gm_out[0, :, 0:384] = gj_own[:, 0:384]
-    r.gm_out[0, :, 384:512] = jnp.zeros((16, 128), F32)
-    r.gm_out[1, :, 0:128] = gj_own[:, 384:512]
-    r.gm_out[1, :, 128:512] = jnp.zeros((16, 384), F32)
-    gm_t = trade_t(wire, place, r.gm_out, r.gm_in)
-    r.gm_in[t] = r.gm_out[t]
-    for k in range(4):
-        r.gj_out[k] = gj_own[4 * k : 4 * k + 4, :]
-    gj_t = trade_t(wire, place, r.gj_out, r.gj_in)
-    r.gj_in[t] = r.gj_out[t]
+    arrive(gj_all)
+    gj_own = add_plane(r.gj_chip[place.a, place.b], r.gj_in)
+    r.gm_out[0, :, 0:384] = gj_own.astype(BF)
+    send_newton(0)
+    for k in range(4):
+        r.late_out[k] = gj_own[4 * k : 4 * k + 4, :]
+    late_t = trade_t(wire, place, r.late_out, r.late_in)
+    r.late_in[t] = r.late_out[t]
     arrive(vp_z)
     r.vp[2] = total(r.vp[1], r.vp_z)
     vp_x = [wire.push(r.vp.at[2], r.vp_x.at[k], p) for k, p in enumerate(place.row_x())]
 
-    arrive(gm_t)
-    for k in range(4):
-        lanes = slice(512 * k, 512 * k + 512)
-        value = muon_beta * r.m_old[:, lanes] + r.gm_in[k]
-        r.momentum[c, place.a, place.b, :, lanes] = value.astype(BF)
+    for w in range(4):
+
+        @pl.when(t == w)
+        def _(w=w):
+            width = gm_widths[w]
+            for sender in range(4):
+                if sender != w:
+                    to_newton(w, sender).wait_recv()
+            for k in range(4):
+                lanes = slice(width * k, width * k + width)
+                value = muon_beta * r.m_old[:, lanes] + r.gm_in[k, :, 0:width].astype(F32)
+                if width * k < 1536:
+                    r.momentum[c, place.a, place.b, :, lanes] = value.astype(BF)
+                else:
+                    r.extra[c, place.a, place.b] = value.astype(BF)
+            if w == 1:
+                r.momentum[c, place.a, place.b, :, 512:1536] = jnp.zeros((16, 1024), BF)
+
     m_b = spread_b(wire, place, r.momentum)
 
-    arrive(gf_t)
-    for k in range(4):
-        part = r.gf_in[k]
+    extra_first = wire.block(16)
+
+    def extra_copies():
+        block = r.extra.at[c, place.a, place.b]
+        copies = []
+        for k, (a, b) in enumerate(place.plane()):
+            copies.append(
+                wire.offer(extra_first, block, block, k, k, place.at_ab(a, b))
+            )
+        return copies
+
+    def extra_swap():
+        block = r.extra.at[c]
+        return wire.offer(extra_first, block, block, 15, 15, sibling)
+
+    @pl.when(t >= 2)
+    def _():
+        for copy in extra_copies():
+            copy.start()
+
+    arrive(early_t)
+    for k in range(4):
+        part = r.early_in[k]
         r.g_expand[:, 512 * k : 512 * k + 512] = part[:, 0:512]
         r.g_reduce[:, 512 * k : 512 * k + 512] = part[:, 512:1024]
-    arrive(gj_t)
-    for k in range(4):
-        lanes = slice(128 * k, 128 * k + 128)
-        part = r.gj_in[k]
-        unpair(r.g_joint, part, k)
-        r.g_output[:, lanes] = part[:, 384:512]
+        r.g_output[:, 128 * k : 128 * k + 128] = part[:, 1024:1152]
+    arrive(late_t)
+    for k in range(4):
+        unpair(r.g_joint, r.late_in[k], k)
     for old, grad, new in (
         (r.m_joint_v, r.g_joint, r.n_joint),
         (r.m_output_v, r.g_output, r.n_output),
@@ -1043,33 +1149,67 @@
     r.vector_next[...] = r.vectors_v[...] - vector_rate * first_hat / (
         jnp.sqrt(second_hat) + adam_epsilon
     )
+    @pl.when(t >= 2)
+    def _():
+        for copy in extra_copies():
+            copy.wait_recv()
+        extra_swap().start()
+        extra_swap().wait_recv()
+
     arrive(m_swaps)
 
     high, small = newton(r, place)
-    for k in range(4):
+    for k in range(3):
         lanes = slice(512 * k, 512 * k + 512)
         columns = r.momentum[:, :, :, :, lanes].reshape(512, 512)
         r.m_rows[:, lanes] = dot(high, columns) + dot(small, columns)
-    for k in range(4):
-        r.u_out[k] = r.m_rows[4 * k : 4 * k + 4, :]
+
+    @pl.when(t >= 2)
+    def _():
+        columns = r.extra[...].reshape(512, 512)
+        r.m_rows[:, 1536:2048] = dot(high, columns) + dot(small, columns)
+
+    @pl.when(t < 2)
+    def _():
+        r.m_rows[:, 1536:2048] = jnp.zeros((16, 512), F32)
+
+    for k in range(4):
+        for p in range(4):
+            r.u_rows[k, 4 * p : 4 * p + 4, :] = r.m_rows[
+                4 * k : 4 * k + 4, 512 * p : 512 * p + 512
+            ]
+    r.u_out[...] = r.u_rows[...].astype(BF)
     u_t = trade_t(wire, place, r.u_out, r.u_in)
     r.u_in[t] = r.u_out[t]
     arrive(u_t)
-    for k in range(4):
-        lanes = slice(128 * k, 128 * k + 128)
-        unpair(r.u_joint, r.u_in[0, :, 512 * k : 512 * k + 384], k)
-        r.u_output[:, lanes] = r.u_in[1, :, 512 * k : 512 * k + 128]
+    r.u_rows[...] = r.u_in[...].astype(F32)
+    for k in range(4):
+        for p in range(4):
+            r.u_wide[k, :, 512 * p : 512 * p + 512] = r.u_rows[k, 4 * p : 4 * p + 4, :]
+    for k in range(4):
+        unpair(r.u_joint, r.u_wide[0, :, 384 * k : 384 * k + 384], k)
     for k, (old, change, new) in enumerate(
         (
             (r.joint_v, r.u_joint, r.u_joint),
-            (r.output_v, r.u_output, r.u_output),
-            (r.expand_v, r.u_in.at[2], r.u_expand),
-            (r.reduce_v, r.u_in.at[3], r.u_reduce),
+            (r.output_v, r.u_wide.at[1, :, pl.ds(0, 512)], r.u_output),
+            (r.expand_v, r.u_wide.at[2], r.u_expand),
+            (r.reduce_v, r.u_wide.at[3], r.u_reduce),
         )
     ):
         factor = muon_rate * 0.2 * math.sqrt(max(D, WIDTHS[k]))
         new[...] = old[...] * (1.0 - muon_rate * muon_decay) - factor * change[...]
     wire.drain()
+    for w in range(4):
+
+        @pl.when(t != w)
+        def _(w=w):
+            to_newton(w, t).wait_send()
+
+    @pl.when(t >= 2)
+    def _():
+        for copy in extra_copies():
+            copy.wait_send()
+        extra_swap().wait_send()
 
 
 def block_stage(*arrays):

time: 119 us -> 108 us (0.908)
  Pallas kernels: 118 us -> 106 us
    pallas_call x1, Pallas kernels: 116 us -> 104 us  [block_stage(): pl.pallas_call(block_kernel, out_shape=tuple((shape(dims, dtype) for _, d...]
where the time goes in v3:
time: 108 us; the launch traced here: 107 us
  Pallas kernels  106 us (98%)
    pallas_call x1, Pallas kernels, block_stage(): pl.pallas_call(block_kernel, out_shape=tuple((shape(dims, dtype) for _, d...  104 us
    pallas_call x1, Pallas kernels, write_stage(): pl.pallas_call(write_kernel, out_shape=tuple((shape(a.shape, a.dtype) for...  2.22 us

profile of v3, /device:TPU:1, one launch (start us, length us, event | category | flops | bytes accessed | tf_op | source)
XLA Modules:
  0.0 107.3 jit_solution(10682285563041526570)
XLA Ops:
  0.7 104.3 %block.1 = (f32[4,1536]{1,0:T(4,128)}, f32[4,512]{1,0:T(4,128)}, f32[4,2048]{1,0:T(4,128)}, f32[4,2048]{1,0:T(4,128)}, f32[4,1536]{1,0:T(4,128)}, /*index=5*/f32...) custom-call(s32[1,4]{1,0:T(1,128)} %refs_0_.1, ...), custom_call_target="tpu_custom_call" | custom-call | tf_op jit(solution)/shard_map/block/pallas_call | solution.py:1216
  104.9 2.2 %write.1 = (f32[4,1536]{1,0:T(4,128)}, f32[4,512]{1,0:T(4,128)}, f32[4,2048]{1,0:T(4,128)}, f32[4,2048]{1,0:T(4,128)}, f32[4,1536]{1,0:T(4,128)}, /*index=5*/f32...) custom-call(f32[4,1536]{1,0:T(4,128)} %get-tuple-element.51.refs_0_,, ...), custom_call_target="tpu_custom_call" | custom-call | tf_op jit(solution)/shard_map/write/pallas_call | solution.py:1248
